TPU v7x, 128 devices: a whole 4x4x4 slice. The times are simulated.
128 devices in a mesh: chan: 16 (over y, z_lo, core), row: 8 (over z_hi, x).
Axes of the slice: x: 4, y: 4, z: 4 (z_hi: 2, z_lo: 2; z = z_hi * 2 + z_lo), core: 2. Of those that a mesh axis runs over, the one named last changes fastest.
Arguments:
- pair: bfloat16 [1280, 1280, 128], P('row', 'chan'), may hold values from -6 to 6
- in_gain: float32 [128], replicated, may hold values from 0.1 to 1.9
- in_bias: float32 [128], replicated, may hold values from -3 to 3
- edge_weight: bfloat16 [128, 512], replicated, may hold values from -0.5 to 0.5
- gate_weight: bfloat16 [128, 128], replicated, may hold values from -0.5 to 0.5
- out_gain: float32 [128], replicated, may hold values from 0.1 to 1.9
- out_bias: float32 [128], replicated, may hold values from -3 to 3
- out_weight: bfloat16 [128, 128], replicated, may hold values from -0.5 to 0.5
Outputs:
- update: bfloat16 [1280, 1280, 128], P('row', 'chan')
All inputs are finite; a program needn't handle non-finite values.
Results may differ from a plain program's by a relative error of at most 0.012.
Values may be sent and summed in bfloat16 or wider, within the bound.
No kernel may reach another device: no remote copies, remote signals or barrier semaphores. Data moves between devices by JAX's collectives and lax.ppermute only.
A program may use at most 128 MiB of HBM per device.

v0:
```python
import jax
import jax.numpy as jnp
from jax import lax
from jax.sharding import PartitionSpec as P


def layer_norm(values, gain, bias, axis):
    mean = jnp.mean(values, axis=axis, keepdims=True)
    centred = values - mean
    var = jnp.mean(centred * centred, axis=axis, keepdims=True)
    return centred * lax.rsqrt(var + 1e-05) * gain + bias


def shards(pair, in_gain, in_bias, edge_weight, gate_weight, out_gain, out_bias, out_weight):
    width = out_weight.shape[0]
    normed = layer_norm(pair.astype(jnp.float32), in_gain, in_bias, -1).astype(jnp.bfloat16)

    def project(index):
        return jnp.einsum(
            "pqc,ch->hpq",
            normed,
            edge_weight[:, index * width : (index + 1) * width],
            preferred_element_type=jnp.float32,
        )

    left = (jax.nn.sigmoid(project(1)) * project(0)).astype(jnp.bfloat16)
    right = (jax.nn.sigmoid(project(3)) * project(2)).astype(jnp.bfloat16)
    gate = jax.nn.sigmoid(
        jnp.einsum("pqc,cd->pqd", normed, gate_weight, preferred_element_type=jnp.float32)
    ).astype(jnp.bfloat16)
    left_group = lax.all_to_all(left, "chan", split_axis=0, concat_axis=2, tiled=True)
    right_group = lax.all_to_all(right, "chan", split_axis=0, concat_axis=2, tiled=True)
    tri = jnp.einsum(
        "cik,cjk->cij",
        left_group,
        lax.all_gather(right_group, "row", axis=1, tiled=True),
        preferred_element_type=jnp.float32,
    ).astype(jnp.bfloat16)
    tri_block = lax.all_to_all(tri, "chan", split_axis=2, concat_axis=0, tiled=True)
    tri_normed = layer_norm(
        tri_block.astype(jnp.float32), out_gain[:, None, None], out_bias[:, None, None], 0
    ).astype(jnp.bfloat16)
    projected = jnp.einsum(
        "hpq,hc->pqc", tri_normed, out_weight, preferred_element_type=jnp.float32
    )
    return (gate.astype(jnp.float32) * projected).astype(jnp.bfloat16)


def solution(mesh):
    return jax.shard_map(
        shards,
        mesh=mesh,
        in_specs=(P("row", "chan", None), P(), P(), P(), P(), P(), P(), P()),
        out_specs=P("row", "chan", None),
        check_vma=False,
    )
```

profile of v0, /device:TPU:1, one launch (start us, length us, event | category | flops | bytes accessed | tf_op | source)
XLA Modules:
  0.0 575.5 jit_solution(1449734368154571508)
XLA Ops:
  6.6 3.6 convert_reduce_fusion
  10.2 5.9 %fusion.8 = f32[160,80]{1,0:T(8,128)S(1)} fusion(bf16[160,80,128]{2,1,0:T(8,128)(2,1)} %param.8, f32[160,80]{1,0:T(8,128)S(1)} %broadcast_multiply_fusion.1), kind=kLoop, calls=%fused_computation.13 | loop fusion | flops 6540800 | bytes 3379200 | tf_op jit(solution)/shard_map/reduce_sum | solution.py:10
  16.2 3.6 fusion.18
  19.8 6.9 %fusion.15 = bf16[128,160,80]{0,2,1:T(8,128)(2,1)} fusion(f32[160,80,128]{2,1,0:T(8,128)S(1)} %fusion.18, bf16[128,512]{1,0:T(8,128)(2,1)S(1)} %copy-done.4, bf16[160,80,128]{2,1,0:T(8,128)(2,1)S(1)} %copy-done.2, f32[128]{0:T(128)S(1)} %copy-done.5, f32[128]{0:T(128)S(1)} %copy-done.6, f32[160,80]{1,0:T(8,128)S(1)} %add_rsqrt_fusion.1, ...), kind=kOutput, calls=%fused_computation.25 | convolution fusion | flops 437452800 | bytes 13304832 | tf_op jit(solution)/shard_map/pqc,ch->hpq/dot_general | solution.py:19
  26.6 7.4 %copy.20 = bf16[128,160,80]{2,1,0:T(8,128)(2,1)} copy(bf16[128,160,80]{0,2,1:T(8,128)(2,1)} %fusion.15) | data formatting | bytes 6553600 | tf_op jit(solution)/shard_map/convert_element_type | solution.py:27
  34.0 67.5 %all_to_all.45 = bf16[128,160,80]{2,1,0:T(8,128)(2,1)S(1)} all-to-all(bf16[128,160,80]{2,1,0:T(8,128)(2,1)} %copy.20), channel_id=1, replica_groups=mesh['chan'=16,'row'=8] {'chan'}, dimensions={0} | all-to-all | bytes 6553600 | tf_op jit(solution)/shard_map/all_to_all | solution.py:32
  101.5 5.7 copy.21
  107.2 9.1 %all_to_all.40 = bf16[8,160,1280]{2,1,0:T(8,128)(2,1)} reshape(bf16[8,160,16,80]{3,2,1,0:T(8,128)(2,1)} %copy.21) | data formatting | bytes 6553600 | tf_op jit(solution)/shard_map/all_to_all | solution.py:32
  116.4 4.3 fusion.21
  120.7 7.6 %fusion.14 = bf16[128,160,80]{0,2,1:T(8,128)(2,1)} fusion(f32[160,80,128]{2,1,0:T(8,128)S(1)} %fusion.21, bf16[128,512]{1,0:T(8,128)(2,1)} %param.11, bf16[160,80,128]{2,1,0:T(8,128)(2,1)S(1)} %copy-done.2, f32[128]{0:T(128)S(1)} %copy-done.5, f32[128]{0:T(128)S(1)} %copy-done.6, f32[160,80]{1,0:T(8,128)S(1)} %add_rsqrt_fusion.1, ...), kind=kOutput, calls=%fused_computation.24 | convolution fusion | flops 437452800 | bytes 13243392 | tf_op jit(solution)/shard_map/pqc,ch->hpq/dot_general | solution.py:19
  128.4 7.6 %copy.18 = bf16[128,160,80]{2,1,0:T(8,128)(2,1)} copy(bf16[128,160,80]{0,2,1:T(8,128)(2,1)} %fusion.14) | data formatting | bytes 6553600 | tf_op jit(solution)/shard_map/convert_element_type | solution.py:26
  135.9 78.4 %all_to_all.46 = bf16[128,160,80]{2,1,0:T(8,128)(2,1)S(1)} all-to-all(bf16[128,160,80]{2,1,0:T(8,128)(2,1)} %copy.18), channel_id=1, replica_groups=mesh['chan'=16,'row'=8] {'chan'}, dimensions={0} | all-to-all | bytes 6553600 | tf_op jit(solution)/shard_map/all_to_all | solution.py:31
  214.3 5.8 %copy.19 = bf16[8,160,16,80]{3,2,1,0:T(8,128)(2,1)} copy(bf16[8,160,16,80]{3,1,0,2:T(8,128)(2,1)S(1)} %bitcast.55) | data formatting | bytes 6553600 | tf_op jit(solution)/shard_map/all_to_all | solution.py:31
  220.1 7.9 %all_to_all.36 = bf16[8,160,1280]{2,1,0:T(8,128)(2,1)S(1)} reshape(bf16[8,160,16,80]{3,2,1,0:T(8,128)(2,1)} %copy.19) | data formatting | bytes 6553600 | tf_op jit(solution)/shard_map/all_to_all | solution.py:31
  227.9 217.3 %all-gather.2.cloned.1.call-done = bf16[8,1280,1280]{2,1,0:T(8,128)(2,1)} async-done(((bf16[8,160,1280]{2,1,0:T(8,128)(2,1)}), bf16[8,1280,1280]{2,1,0:T(8,128)(2,1)}) %all-gather.2.cloned.1.call-update) | async-done | bytes 26214416 | tf_op jit(solution)/shard_map/all_gather | solution.py:36
  445.3 14.7 %convolution_convert_fusion = bf16[8,160,1280]{2,1,0:T(8,128)(2,1)} fusion(bf16[8,160,1280]{2,1,0:T(8,128)(2,1)S(1)} %all_to_all.36, bf16[8,1280,1280]{2,1,0:T(8,128)(2,1)} %all-gather.2.cloned.1.call-done), kind=kOutput, calls=%fused_computation.23 | convolution fusion | flops 4195942400 | bytes 32768000 | tf_op jit(solution)/shard_map/cik,cjk->cij/dot_general | solution.py:33
  460.0 8.7 %copy.22 = bf16[8,160,1280]{1,0,2:T(8,128)(2,1)} copy(bf16[8,160,1280]{2,1,0:T(8,128)(2,1)} %convolution_convert_fusion) | data formatting | bytes 6553600 | tf_op jit(solution)/shard_map/convert_element_type | solution.py:38
  468.7 65.8 %all_to_all.47 = bf16[8,160,1280]{1,0,2:T(8,128)(2,1)} all-to-all(bf16[8,160,1280]{1,0,2:T(8,128)(2,1)} %copy.22), channel_id=1, replica_groups=mesh['chan'=16,'row'=8] {'chan'}, dimensions={2} | all-to-all | bytes 6553600 | tf_op jit(solution)/shard_map/all_to_all | solution.py:39
  534.4 9.8 %copy.23 = f32[8,160,16,80]{3,1,0,2:T(8,128)} copy(bf16[8,160,16,80]{1,0,3,2:T(8,128)(2,1)} %bitcast.56) | data formatting | bytes 9830400 | tf_op jit(solution)/shard_map/convert_element_type | solution.py:41
  544.2 4.9 bitcast_reduce_fusion
  549.1 2.0 copy-done.1
  552.6 4.2 fusion.3
  556.8 4.9 fusion.12
  561.7 7.0 %multiply_convert_fusion.2 = bf16[160,80,128]{2,1,0:T(8,128)(2,1)} fusion(f32[160,80,128]{2,1,0:T(8,128)S(1)} %fusion.12, bf16[128,128]{1,0:T(8,128)(2,1)S(1)} %copy-done.9, bf16[160,80,128]{2,1,0:T(8,128)(2,1)S(1)} %copy-done.3, f32[128]{0:T(128)S(1)} %copy-done.5, f32[128]{0:T(128)S(1)} %copy-done.6, f32[160,80]{1,0:T(8,128)S(1)} %add_rsqrt_fusion.1, ...), kind=kOutput, calls=%fused_computation.19 | convolution fusion | flops 440729600 | bytes 13243392 | tf_op jit(solution)/shard_map/pqc,cd->pqd/dot_general | solution.py:29
  (26 shorter events, 1.6 us)
Async XLA Ops:
  6.5 550.3 %copy-start = (bf16[128,128]{1,0:T(8,128)(2,1)S(1)}, bf16[128,128]{1,0:T(8,128)(2,1)}, u32[]{:S(2)}) copy-start(bf16[128,128]{1,0:T(8,128)(2,1)} %param.15) | copy-start | bytes 98308
  6.5 9.6 %copy-start.2 = (bf16[160,80,128]{2,1,0:T(8,128)(2,1)S(1)}, bf16[160,80,128]{2,1,0:T(8,128)(2,1)}, u32[]{:S(2)}) copy-start(bf16[160,80,128]{2,1,0:T(8,128)(2,1)} %param.8) | copy-start | bytes 9830404
  6.5 9.6 %copy-start.5 = (f32[128]{0:T(128)S(1)}, f32[128]{0:T(128)}, u32[]{:S(2)}) copy-start(f32[128]{0:T(128)} %param.10) | copy-start | bytes 1540
  6.5 9.6 %copy-start.6 = (f32[128]{0:T(128)S(1)}, f32[128]{0:T(128)}, u32[]{:S(2)}) copy-start(f32[128]{0:T(128)} %param.9) | copy-start | bytes 1540
  6.5 438.7 %all-gather.2.cloned.1.call-start = ((), (), s32[]{:S(2)}) async-start(), calls=%async_computation.3 | async-start | bytes 29491200 | tf_op jit(solution)/shard_map/all_gather | solution.py:36
  6.6 9.6 %copy-start.4 = (bf16[128,512]{1,0:T(8,128)(2,1)S(1)}, bf16[128,512]{1,0:T(8,128)(2,1)}, u32[]{:S(2)}) copy-start(bf16[128,512]{1,0:T(8,128)(2,1)} %param.11) | copy-start | bytes 393220
  544.2 7.0 %copy-start.1 = (f32[8,160,16,80]{3,1,0,2:T(8,128)S(1)}, f32[8,160,16,80]{3,1,0,2:T(8,128)}, u32[]{:S(2)}) copy-start(f32[8,160,16,80]{3,1,0,2:T(8,128)} %copy.23) | copy-start | bytes 19660804
  549.1 3.5 copy-start.7
  549.1 3.5 copy-start.8
  556.8 4.9 copy-start.3
  556.8 4.9 copy-start.9
Sparse Core Ops, SparseCore 0:
  116.5 328.7 all-gather.1
where the time goes:
time: 577 us; the launch traced here: 576 us
  waiting for transfers between devices  217 us (38%)
  blocking collectives  212 us (37%)
  local copies, waits for them, and re-layouts  63.9 us (11%)
  matrix products  49 us (8%)
  other arithmetic  20.1 us (3%)
  between operations  13.5 us (2%)
    all_gather x1, waiting for transfers between devices, shards(): lax.all_gather(right_group, 'row', axis=1, tiled=True)  217 us
    all_to_all x1, blocking collectives, shards(): lax.all_to_all(left, 'chan', split_axis=0, concat_axis=2, tiled=True)  78.4 us
    all_to_all x1, blocking collectives, shards(): lax.all_to_all(right, 'chan', split_axis=0, concat_axis=2, tiled=True)  67.5 us
    all_to_all x1, blocking collectives, shards(): lax.all_to_all(tri, 'chan', split_axis=2, concat_axis=0, tiled=True)  65.8 us
    dot_general x4, matrix products, project(): jnp.einsum('pqc,ch->hpq', normed, edge_weight[:, index * width:(index + 1...  22.4 us
    all_to_all x2, local copies, waits for them, and re-layouts, shards(): lax.all_to_all(right, 'chan', split_axis=0, concat_axis=2, tiled=True)  14.8 us
    dot_general x1, matrix products, shards(): jnp.einsum('cik,cjk->cij', left_group, lax.all_gather(right_group, 'row',...  14.7 us
    all_to_all x2, local copies, waits for them, and re-layouts, shards(): lax.all_to_all(left, 'chan', split_axis=0, concat_axis=2, tiled=True)  13.6 us
  transfers between devices with their start and end apart: 1, of which 1 were waited for; matrix products, arithmetic and copies ran while one was open for 4% of the time, Pallas kernels for 0%

commit v1 on v0

v1 whole, which is shorter than its diff:
```python
import jax
import jax.numpy as jnp
from jax import lax
from jax.experimental import pallas as pl
from jax.experimental.pallas import tpu as pltpu
from jax.sharding import PartitionSpec as P

ROWS, COLS, C = 160, 80, 128
LANES = 128
REST = ROWS - LANES
PACK = LANES // REST
TAIL = COLS // PACK
CHUNK = 16
BOTH = 2 * (COLS + TAIL)
BACK = 104
N_ROW, N_CHAN = 8, 16
SIDE = 1280
F32, BF16 = jnp.float32, jnp.bfloat16
MIB = 1 << 20


def sigmoid(x):
    return 0.5 * jnp.tanh(0.5 * x) + 0.5


def layer_norm(values, gain, bias, axis):
    mean = jnp.mean(values, axis=axis, keepdims=True)
    centred = values - mean
    var = jnp.mean(centred * centred, axis=axis, keepdims=True)
    return centred * lax.rsqrt(var + 1e-05) * gain + bias


def edges_kernel(pair_ref, gain_ref, bias_ref, weight_ref, out_ref, weight_t, normed, dense, tail):
    step = pl.program_id(0)

    @pl.when(step == 0)
    def _():
        for m in range(4):
            weight_t[m * 128 : (m + 1) * 128, :] = weight_ref[:, m * 128 : (m + 1) * 128].T

    group = 8
    gain, bias = gain_ref[...], bias_ref[...]

    @pl.loop(0, ROWS // group)
    def _(n):
        block = pair_ref[pl.ds(n * group, group)].reshape(group * CHUNK, C).astype(F32)
        at = pl.multiple_of(n * group * CHUNK, group * CHUNK)
        normed[pl.ds(at, group * CHUNK), :] = layer_norm(block, gain, bias, -1)

    def product(x, side):
        both = lax.dot_general(
            weight_t[side * 256 : (side + 1) * 256, :], x, (((1,), (1,)), ((), ())), preferred_element_type=F32
        )
        return sigmoid(both[128:]) * both[:128]

    @pl.loop(0, CHUNK // 2)
    def _(n):
        x = jnp.concatenate(
            [normed[pl.ds(2 * n + e, LANES, stride=CHUNK), :] for e in range(2)], axis=0
        ).astype(BF16)
        for side in range(2):
            value = product(x, side)
            for e in range(2):
                dense[side, pl.ds(2 * n + e, C, stride=CHUNK), :] = value[:, e * 128 : (e + 1) * 128]

    for n in range(2):
        x = jnp.concatenate(
            [
                normed[pl.ds(LANES * CHUNK + 8 * n + e, REST, stride=CHUNK), :]
                for e in range(8)
            ],
            axis=0,
        ).astype(BF16)
        for side in range(2):
            value = product(x, side)
            for e in range(2):
                tail[pl.ds(side * TAIL + 4 * step + 2 * n + e, C, stride=2 * TAIL), :] = value[:, e * 128 : (e + 1) * 128]

    @pl.loop(0, C // 8)
    def _(n):
        at = pl.multiple_of(n * 8 * CHUNK, 8 * CHUNK)
        for side in range(2):
            to = pl.multiple_of(side * COLS + step * CHUNK, CHUNK)
            out_ref[pl.ds(8 * n, 8), pl.ds(to, CHUNK), :] = (
                dense[side, pl.ds(at, 8 * CHUNK), :].reshape(8, CHUNK, LANES).astype(BF16)
            )

    @pl.when(step == COLS // CHUNK - 1)
    def _():
        @pl.loop(0, C // 8)
        def _(n):
            at = pl.multiple_of(n * 16 * TAIL, 16 * TAIL)
            out_ref[pl.ds(8 * n, 8), 2 * COLS :, :] = (
                tail[pl.ds(at, 16 * TAIL), :].reshape(8, 2 * TAIL, LANES).astype(BF16)
            )


def edges(pair, gain, bias, weight):
    return pl.pallas_call(
        edges_kernel,
        grid=(COLS // CHUNK,),
        in_specs=[
            pl.BlockSpec((ROWS, CHUNK, C), lambda t: (0, t, 0)),
            pl.BlockSpec((1, C), lambda t: (0, 0)),
            pl.BlockSpec((1, C), lambda t: (0, 0)),
            pl.BlockSpec((C, 4 * C), lambda t: (0, 0)),
        ],
        out_specs=pl.BlockSpec((C, BOTH, LANES), lambda t: (0, 0, 0)),
        out_shape=jax.ShapeDtypeStruct((C, BOTH, LANES), BF16),
        scratch_shapes=[
            pltpu.VMEM((4 * C, C), BF16),
            pltpu.VMEM((ROWS * CHUNK, C), F32),
            pltpu.VMEM((2, C * CHUNK, LANES), F32),
            pltpu.VMEM((C * 2 * TAIL, LANES), F32),
        ],
        compiler_params=pltpu.CompilerParams(vmem_limit_bytes=40 * MIB),
        cost_estimate=pl.CostEstimate(flops=2 * ROWS * COLS * C * 4 * C, bytes_accessed=10 * MIB, transcendentals=0),
        name="edges",
    )(pair, gain[None, :], bias[None, :], weight)


def regroup(pieces, lane):
    out = []
    for b in range(PACK):
        total = None
        for a in range(PACK):
            shift = ((a - b) * REST) % LANES
            moved = pltpu.roll(pieces[a], shift, 1) if shift else pieces[a]
            total = moved if total is None else jnp.where(lane // REST == a, moved, total)
        out.append(total)
    return out


def triangle_kernel(
    edges_ref, out_ref, left, right, right_t, rest, rest_left, rest_right, tri, tri_rest, packed, sems
):
    loads = []
    for r in range(N_ROW):
        for c in range(N_CHAN):
            s = r * N_CHAN + c
            for side, dst in ((1, right), (0, left)):
                loads.append(
                    pltpu.make_async_copy(
                        edges_ref.at[s, pl.ds(side * COLS, COLS), :],
                        dst.at[pl.ds(c * COLS, COLS), pl.ds(r * LANES, LANES)],
                        sems.at[side],
                    )
                )
    tails = pltpu.make_async_copy(edges_ref.at[:, pl.ds(2 * COLS, 2 * TAIL), :], rest, sems.at[2])
    tails.start()
    for load in loads:
        load.start()
    tails.wait()
    lane = lax.broadcasted_iota(jnp.int32, (2 * TAIL, LANES), 1)

    @pl.loop(0, N_CHAN)
    def _(c):
        for q in range(N_ROW // PACK):
            pieces = [rest[(q * PACK + a) * N_CHAN + c].astype(F32) for a in range(PACK)]
            for b, value in enumerate(regroup(pieces, lane)):
                rest_left[q, pl.ds(c * COLS + b, TAIL, stride=PACK), :] = value[:TAIL]
                rest_right[q, pl.ds(c * COLS + b, TAIL, stride=PACK), :] = value[TAIL:]

    for load in loads:
        load.wait()
    for q in range(N_ROW // PACK):
        left[:, (N_ROW + q) * LANES : (N_ROW + q + 1) * LANES] = rest_left[q].astype(BF16)
    for r in range(N_ROW):
        right_t[r * ROWS : r * ROWS + LANES, :] = right[:, r * LANES : (r + 1) * LANES].T
    for q in range(N_ROW // PACK):
        turned = rest_right[q].astype(BF16).T
        for a in range(PACK):
            at = (q * PACK + a) * ROWS + LANES
            right_t[at : at + REST, :] = turned[a * REST : (a + 1) * REST]

    stores = []
    width = 256
    for n in range(SIDE // width):
        part = jnp.dot(right_t[...], left[:, n * width : (n + 1) * width], preferred_element_type=F32)
        if n < SIDE // width - 1:
            tri[:, n * width : (n + 1) * width] = part.astype(BF16)
            for r in (2 * n, 2 * n + 1):
                for c in range(N_CHAN):
                    store = pltpu.make_async_copy(
                        tri.at[pl.ds(c * COLS, COLS), pl.ds(r * LANES, LANES)],
                        out_ref.at[r * N_CHAN + c, pl.ds(0, COLS), :],
                        sems.at[3],
                    )
                    store.start()
                    stores.append(store)
        else:
            for q in range(N_ROW // PACK):
                tri_rest[q] = part[:, q * LANES : (q + 1) * LANES]

    lane = lax.broadcasted_iota(jnp.int32, (TAIL, LANES), 1)

    @pl.loop(0, N_CHAN)
    def _(c):
        for q in range(N_ROW // PACK):
            pieces = [
                tri_rest[q, pl.ds(c * COLS + b, TAIL, stride=PACK), :] for b in range(PACK)
            ]
            for a, value in enumerate(regroup(pieces, lane)):
                value = jnp.concatenate([value, jnp.zeros((BACK - COLS - TAIL, LANES), F32)], axis=0)
                packed[(q * PACK + a) * N_CHAN + c] = value.astype(BF16)

    store = pltpu.make_async_copy(packed, out_ref.at[:, pl.ds(COLS, BACK - COLS), :], sems.at[4])
    store.start()
    store.wait()
    for store in stores:
        store.wait()


def triangle(edges_all):
    return pl.pallas_call(
        triangle_kernel,
        in_specs=[pl.BlockSpec(memory_space=pl.ANY)],
        out_specs=pl.BlockSpec(memory_space=pl.ANY),
        out_shape=jax.ShapeDtypeStruct((N_ROW * N_CHAN, BACK, LANES), BF16),
        scratch_shapes=[
            pltpu.VMEM((SIDE, SIDE), BF16),
            pltpu.VMEM((SIDE, N_ROW * LANES), BF16),
            pltpu.VMEM((SIDE, SIDE), BF16),
            pltpu.VMEM((N_ROW * N_CHAN, 2 * TAIL, LANES), BF16),
            pltpu.VMEM((N_ROW // PACK, SIDE, LANES), F32),
            pltpu.VMEM((N_ROW // PACK, SIDE, LANES), F32),
            pltpu.VMEM((SIDE, N_ROW * LANES), BF16),
            pltpu.VMEM((N_ROW // PACK, SIDE, LANES), F32),
            pltpu.VMEM((N_ROW * N_CHAN, BACK - COLS, LANES), BF16),
            pltpu.SemaphoreType.DMA((5,)),
        ],
        compiler_params=pltpu.CompilerParams(vmem_limit_bytes=48 * MIB),
        cost_estimate=pl.CostEstimate(flops=2 * SIDE**3, bytes_accessed=10 * MIB, transcendentals=0),
        name="triangle",
    )(edges_all)


def finish_kernel(tri_ref, gate_ref, gain_ref, bias_ref, weight_ref, out_ref, wide, dense, tail):
    step = pl.program_id(0)
    full = COLS // CHUNK
    gain, bias, weight = gain_ref[...], bias_ref[...], weight_ref[...]

    @pl.loop(0, C // 8)
    def _(n):
        at = pl.multiple_of(n * 8 * CHUNK, 8 * CHUNK)
        wide[pl.ds(at, 8 * CHUNK), :] = tri_ref[pl.ds(8 * n, 8)].reshape(8 * CHUNK, LANES).astype(F32)

    def project(g):
        normed = layer_norm(wide[pl.ds(g, C, stride=CHUNK), :], gain, bias, 0).astype(BF16)
        return lax.dot_general(normed, weight, (((0,), (0,)), ((), ())), preferred_element_type=F32)

    @pl.when(step < full)
    def _():
        @pl.loop(0, CHUNK)
        def _(g):
            dense[pl.ds(g, LANES, stride=CHUNK), :] = project(g)

        to = pl.multiple_of(step * CHUNK, CHUNK)

        @pl.loop(0, LANES // 8)
        def _(n):
            at = pl.multiple_of(n * 8 * CHUNK, 8 * CHUNK)
            value = dense[pl.ds(at, 8 * CHUNK), :].reshape(8, CHUNK, C)
            gate = gate_ref[pl.ds(8 * n, 8), pl.ds(to, CHUNK), :].astype(F32)
            out_ref[pl.ds(8 * n, 8), pl.ds(to, CHUNK), :] = (gate * value).astype(BF16)

    @pl.when(step >= full)
    def _():
        first = (step - full) * CHUNK

        @pl.loop(0, jnp.minimum(CHUNK, TAIL - first))
        def _(g):
            value = project(g)
            for e in range(PACK):
                tail[pl.ds(PACK * (first + g) + e, REST, stride=COLS), :] = value[e * REST : (e + 1) * REST]

    @pl.when(step == pl.num_programs(0) - 1)
    def _():
        @pl.loop(0, REST // 8)
        def _(n):
            at = pl.multiple_of(n * 8 * COLS, 8 * COLS)
            value = tail[pl.ds(at, 8 * COLS), :].reshape(8, COLS, C)
            gate = gate_ref[pl.ds(LANES + 8 * n, 8)].astype(F32)
            out_ref[pl.ds(LANES + 8 * n, 8)] = (gate * value).astype(BF16)


def finish(tri, gate, gain, bias, weight):
    steps = COLS // CHUNK + -(-TAIL // CHUNK)
    return pl.pallas_call(
        finish_kernel,
        grid=(steps,),
        in_specs=[
            pl.BlockSpec((C, CHUNK, LANES), lambda t: (0, t, 0)),
            pl.BlockSpec((ROWS, COLS, C), lambda t: (0, 0, 0)),
            pl.BlockSpec((C, 1), lambda t: (0, 0)),
            pl.BlockSpec((C, 1), lambda t: (0, 0)),
            pl.BlockSpec((C, C), lambda t: (0, 0)),
        ],
        out_specs=pl.BlockSpec((ROWS, COLS, C), lambda t: (0, 0, 0)),
        out_shape=jax.ShapeDtypeStruct((ROWS, COLS, C), BF16),
        scratch_shapes=[
            pltpu.VMEM((C * CHUNK, LANES), F32),
            pltpu.VMEM((LANES * CHUNK, C), F32),
            pltpu.VMEM((REST * COLS, C), F32),
        ],
        compiler_params=pltpu.CompilerParams(vmem_limit_bytes=40 * MIB),
        cost_estimate=pl.CostEstimate(flops=2 * ROWS * COLS * C * C, bytes_accessed=10 * MIB, transcendentals=0),
        name="finish",
    )(tri, gate, gain[:, None], bias[:, None], weight)


def shards(pair, in_gain, in_bias, edge_weight, gate_weight, out_gain, out_bias, out_weight):
    both = edges(pair, in_gain, in_bias, edge_weight)
    both_all = lax.all_to_all(both, ("row", "chan"), split_axis=0, concat_axis=0, tiled=True)
    normed = layer_norm(pair.astype(F32), in_gain, in_bias, -1).astype(BF16)
    gate = jax.nn.sigmoid(
        jnp.einsum("pqc,cd->pqd", normed, gate_weight, preferred_element_type=F32)
    ).astype(BF16)
    tri = lax.all_to_all(triangle(both_all), ("row", "chan"), split_axis=0, concat_axis=0, tiled=True)
    return finish(tri, gate, out_gain, out_bias, out_weight)


def solution(mesh):
    return jax.shard_map(
        shards,
        mesh=mesh,
        in_specs=(P("row", "chan", None), P(), P(), P(), P(), P(), P(), P()),
        out_specs=P("row", "chan", None),
        check_vma=False,
    )
```

time: 577 us -> 232 us (0.40)
  waiting for transfers between devices: 217 us -> 30.3 us
  blocking collectives: 212 us -> 90.8 us
  Pallas kernels: 0 us -> 84.1 us
  local copies, waits for them, and re-layouts: 63.9 us -> 8.09 us
  matrix products: 49 us -> 6.93 us
  other arithmetic: 20.1 us -> 6.41 us
  between operations: 13.5 us -> 0.13 us
    all_gather x1 -> x0, waiting for transfers between devices: 217 us -> none  [shards(): lax.all_gather(right_group, 'row', axis=1, tiled=True)]
    all_to_all x3 -> x1, blocking collectives: 212 us -> 90.8 us  [shards(): lax.all_to_all(both, ('row', 'chan'), split_axis=0, concat_axis=0, tiled=...]
    pallas_call x0 -> x3, Pallas kernels: none -> 84.1 us  [the longest x1 35 us: finish(): pl.pallas_call(finish_kernel, grid=(steps,), in_specs=[pl.BlockSpec((C, C...]
    dot_general x7 -> x1, matrix products: 49 us -> 6.93 us  [shards(): jnp.einsum('pqc,cd->pqd', normed, gate_weight, preferred_element_type=F32)]
    convert_element_type x4 -> x0, local copies, waits for them, and re-layouts: 33.4 us -> none  [the longest x1 9.76 us: shards(): tri_block.astype(jnp.float32)]
    all_to_all x0 -> x1, waiting for transfers between devices: none -> 30.3 us  [shards(): lax.all_to_all(triangle(both_all), ('row', 'chan'), split_axis=0, concat_...]
    all_to_all x4 -> x0, local copies, waits for them, and re-layouts: 28.4 us -> none  [the longest x2 14.8 us: shards(): lax.all_to_all(right, 'chan', split_axis=0, concat_axis=2, tiled=True)]
    reduce_sum x2 -> x1, other arithmetic: 8.44 us -> 1.47 us  [layer_norm(): mean = jnp.mean(values, axis=axis, keepdims=True)]
  transfers between devices with their start and end apart: 1 -> 1, of which waited for: 1 -> 1; matrix products, arithmetic and copies ran while one was open for 4% -> 6% of each run, Pallas kernels for 0% -> 0%
where the time goes in v1:
time: 232 us
  blocking collectives  90.8 us (39%)
  Pallas kernels  84.1 us (36%)
  waiting for transfers between devices  30.3 us (13%)
  local copies, waits for them, and re-layouts  8.09 us (3%)
  matrix products  6.93 us (3%)
  other arithmetic  6.41 us (3%)
  starting transfers between devices  5.42 us (2%)
    all_to_all x1, blocking collectives, shards(): lax.all_to_all(both, ('row', 'chan'), split_axis=0, concat_axis=0, tiled=...  90.8 us
    pallas_call x1, Pallas kernels, finish(): pl.pallas_call(finish_kernel, grid=(steps,), in_specs=[pl.BlockSpec((C, C...  35 us
    pallas_call x1, Pallas kernels, edges(): pl.pallas_call(edges_kernel, grid=(COLS // CHUNK,), in_specs=[pl.BlockSpe...  34 us
    all_to_all x1, waiting for transfers between devices, shards(): lax.all_to_all(triangle(both_all), ('row', 'chan'), split_axis=0, concat_...  30.3 us
    pallas_call x1, Pallas kernels, triangle(): pl.pallas_call(triangle_kernel, in_specs=[pl.BlockSpec(memory_space=pl.AN...  15.1 us
    unnamed x26, local copies, waits for them, and re-layouts  7.87 us
    dot_general x1, matrix products, shards(): jnp.einsum('pqc,cd->pqd', normed, gate_weight, preferred_element_type=F32)  6.93 us
    all_to_all x1, starting transfers between devices, shards(): lax.all_to_all(triangle(both_all), ('row', 'chan'), split_axis=0, concat_...  5.42 us
  transfers between devices with their start and end apart: 1, of which 1 were waited for; matrix products, arithmetic and copies ran while one was open for 6% of the time, Pallas kernels for 0%

profile of v1, /device:TPU:1, one launch (start us, length us, event | category | flops | bytes accessed | tf_op | source)
XLA Modules:
  0.0 232.1 jit_solution(14399793173167506698)
XLA Ops:
  0.0 0.0 copy-start
  0.0 1.9 copy-done.1
  1.9 0.9 copy-done.5
  2.8 0.7 copy-done.7
  3.5 0.7 copy-done.9
  4.2 34.0 %edges.1 = bf16[128,200,128]{2,1,0:T(8,128)(2,1)S(1)} custom-call(bf16[160,80,128]{2,1,0:T(8,128)(2,1)S(1)} %copy-done.1, f32[1,128]{1,0:T(1,128)S(1)} %bitcast.7, f32[1,128]{1,0:T(1,128)S(1)} %bitcast.8, bf16[128,512]{1,0:T(8,128)(2,1)S(1)} %copy-done.5), custom_call_target="tpu_custom_call" | custom-call | flops 1677721600 | bytes 10485760 | tf_op jit(solution)/shard_map/edges/pallas_call | solution.py:99
  38.1 90.8 %all_to_all.10.edges_ref = bf16[128,200,128]{2,1,0:T(8,128)(2,1)} all-to-all(bf16[128,200,128]{2,1,0:T(8,128)(2,1)S(1)} %edges.1), channel_id=1, replica_groups=mesh['chan'=16,'row'=8] {'row','chan'}, dimensions={0} | all-to-all | bytes 13107200 | tf_op jit(solution)/shard_map/all_to_all | solution.py:314
  128.9 15.1 %triangle.1 = bf16[128,104,128]{2,1,0:T(8,128)(2,1)S(1)} custom-call(bf16[128,200,128]{2,1,0:T(8,128)(2,1)} %all_to_all.10.edges_ref), custom_call_target="tpu_custom_call" | custom-call | flops 4194304000 | bytes 10485760 | tf_op jit(solution)/shard_map/triangle/pallas_call | solution.py:215
  144.0 0.0 copy-start.3
  144.0 1.8 copy-done.3
  145.8 0.0 copy-start.10
  145.8 5.4 %all-to-all-start.1 = ((bf16[128,104,128]{2,1,0:T(8,128)(2,1)}), bf16[128,104,128]{2,1,0:T(8,128)(2,1)}, u32[]{:S(2)}, u32[]{:S(2)}) async-start(bf16[128,104,128]{2,1,0:T(8,128)(2,1)} %copy-done.3), calls=%async_computation.1 | async-start | bytes 6815744 | tf_op jit(solution)/shard_map/all_to_all | solution.py:319
  151.2 0.0 copy-done.11
  151.2 0.1 copy.9.gain_ref
  151.4 0.0 copy-done.12
  151.4 0.1 copy.10.bias_ref
  151.5 0.0 copy-done.2
  151.5 1.5 convert_reduce_fusion
  153.0 4.9 %fusion.2 = f32[160,80]{1,0:T(8,128)S(1)} fusion(bf16[160,80,128]{2,1,0:T(8,128)(2,1)S(1)} %copy-done.2, f32[160,80]{1,0:T(8,128)S(1)} %broadcast_multiply_fusion), kind=kLoop, calls=%fused_computation.4 | loop fusion | flops 6540800 | bytes 3379200 | tf_op jit(solution)/shard_map/reduce_sum | solution.py:29
  157.9 0.0 copy-start.6
  158.0 6.9 %divide_convert_fusion.gate_ref = bf16[160,80,128]{2,1,0:T(8,128)(2,1)} fusion(bf16[160,80,128]{2,1,0:T(8,128)(2,1)S(1)} %copy-done.2, f32[128]{0:T(128)S(1)} %copy-done.10, f32[128]{0:T(128)S(1)} %copy-done.8, f32[160,80]{1,0:T(8,128)S(1)} %add_rsqrt_fusion, f32[160,80]{1,0:T(8,128)S(1)} %broadcast_multiply_fusion, bf16[128,128]{1,0:T(8,128)(2,1)S(1)} %copy-done), kind=kOutput, calls=%fused_computation.8 | convolution fusion | flops 435814400 | bytes 6689792 | tf_op jit(solution)/shard_map/pqc,cd->pqd/dot_general | solution.py:317
  164.9 30.3 %all-to-all-done.1.tri_ref = bf16[128,104,128]{2,1,0:T(8,128)(2,1)} async-done(((bf16[128,104,128]{2,1,0:T(8,128)(2,1)}), bf16[128,104,128]{2,1,0:T(8,128)(2,1)}, u32[]{:S(2)}, u32[]{:S(2)}) %all-to-all-start.1) | async-done | bytes 3407904 | tf_op jit(solution)/shard_map/all_to_all | solution.py:319
  195.2 1.9 copy-done.4
  197.1 35.0 %finish.1 = bf16[160,80,128]{2,1,0:T(8,128)(2,1)} custom-call(bf16[128,104,128]{2,1,0:T(8,128)(2,1)} %all-to-all-done.1.tri_ref, bf16[160,80,128]{2,1,0:T(8,128)(2,1)S(1)} %copy-done.4, f32[128,1]{1,0:T(8,128)S(1)} %copy.9.gain_ref, f32[128,1]{1,0:T(8,128)S(1)} %copy.10.bias_ref, bf16[128,128]{1,0:T(8,128)(2,1)S(1)} %copy-done.6), custom_call_target="tpu_custom_call" | custom-call | flops 419430400 | bytes 10485760 | tf_op jit(solution)/shard_map/finish/pallas_call | solution.py:289
  (15 shorter events, 0.1 us)
Async XLA Ops:
  0.0 157.9 %copy-start = (bf16[128,128]{1,0:T(8,128)(2,1)S(1)}, bf16[128,128]{1,0:T(8,128)(2,1)}, u32[]{:S(2)}) copy-start(bf16[128,128]{1,0:T(8,128)(2,1)} %param.12) | copy-start | bytes 98308
  0.0 1.9 copy-start.1
  1.9 0.9 copy-start.5
  2.8 0.7 copy-start.7
  3.5 0.7 copy-start.9
  144.0 1.8 copy-start.3
  145.8 5.5 %copy-start.11 = (f32[128]{0:T(128)S(1)}, f32[128]{0:T(128)}, u32[]{:S(2)}) copy-start(f32[128]{0:T(128)} %param.13) | copy-start | bytes 1540
  145.8 5.6 %copy-start.12 = (f32[128]{0:T(128)S(1)}, f32[128]{0:T(128)}, u32[]{:S(2)}) copy-start(f32[128]{0:T(128)} %param.14) | copy-start | bytes 1540
  145.8 5.7 %copy-start.2 = (bf16[160,80,128]{2,1,0:T(8,128)(2,1)S(1)}, bf16[160,80,128]{2,1,0:T(8,128)(2,1)}, u32[]{:S(2)}) copy-start(bf16[160,80,128]{2,1,0:T(8,128)(2,1)} %pair_ref.1) | copy-start | bytes 9830404
  145.8 12.1 %copy-start.8 = (f32[128]{0:T(128)S(1)}, f32[128]{0:T(128)}, u32[]{:S(2)}) copy-start(f32[128]{0:T(128)} %param.9) | copy-start | bytes 1540
  145.8 12.1 %copy-start.10 = (f32[128]{0:T(128)S(1)}, f32[128]{0:T(128)}, u32[]{:S(2)}) copy-start(f32[128]{0:T(128)} %param.10) | copy-start | bytes 1540
  145.8 49.4 %all-to-all-start.1 = ((bf16[128,104,128]{2,1,0:T(8,128)(2,1)}), bf16[128,104,128]{2,1,0:T(8,128)(2,1)}, u32[]{:S(2)}, u32[]{:S(2)}) async-start(bf16[128,104,128]{2,1,0:T(8,128)(2,1)} %copy-done.3), calls=%async_computation.1 | async-start | bytes 6815744 | tf_op jit(solution)/shard_map/all_to_all | solution.py:319
  157.9 37.2 %copy-start.6 = (bf16[128,128]{1,0:T(8,128)(2,1)S(1)}, bf16[128,128]{1,0:T(8,128)(2,1)}, u32[]{:S(2)}) copy-start(bf16[128,128]{1,0:T(8,128)(2,1)} %weight_ref.3) | copy-start | bytes 98308
  195.2 1.9 copy-start.4

commit v2 on v1

--- a/solution.py
+++ b/solution.py
@@ -11,12 +11,14 @@
 PACK = LANES // REST
 TAIL = COLS // PACK
 CHUNK = 16
+CHUNKS = COLS // CHUNK
 BOTH = 2 * (COLS + TAIL)
 BACK = 104
 N_ROW, N_CHAN = 8, 16
 SIDE = 1280
 F32, BF16 = jnp.float32, jnp.bfloat16
 MIB = 1 << 20
+VMEM_BYTES = 60 * MIB
 
 
 def sigmoid(x):
@@ -30,22 +32,15 @@
     return centred * lax.rsqrt(var + 1e-05) * gain + bias
 
 
-def edges_kernel(pair_ref, gain_ref, bias_ref, weight_ref, out_ref, weight_t, normed, dense, tail):
-    step = pl.program_id(0)
-
-    @pl.when(step == 0)
-    def _():
-        for m in range(4):
-            weight_t[m * 128 : (m + 1) * 128, :] = weight_ref[:, m * 128 : (m + 1) * 128].T
-
-    group = 8
+def edges_kernel(pair_ref, gain_ref, bias_ref, weight_ref, out_ref, weight_t, held, normed, dense, tail, done, sems):
+    loads = [
+        pltpu.make_async_copy(pair_ref.at[:, pl.ds(t * CHUNK, CHUNK), :], held.at[t], sems.at[t]) for t in range(CHUNKS)
+    ]
+    for load in loads:
+        load.start()
+    for m in range(4):
+        weight_t[m * 128 : (m + 1) * 128, :] = weight_ref[:, m * 128 : (m + 1) * 128].T
     gain, bias = gain_ref[...], bias_ref[...]
-
-    @pl.loop(0, ROWS // group)
-    def _(n):
-        block = pair_ref[pl.ds(n * group, group)].reshape(group * CHUNK, C).astype(F32)
-        at = pl.multiple_of(n * group * CHUNK, group * CHUNK)
-        normed[pl.ds(at, group * CHUNK), :] = layer_norm(block, gain, bias, -1)
 
     def product(x, side):
         both = lax.dot_general(
@@ -53,67 +48,72 @@
         )
         return sigmoid(both[128:]) * both[:128]
 
-    @pl.loop(0, CHUNK // 2)
-    def _(n):
-        x = jnp.concatenate(
-            [normed[pl.ds(2 * n + e, LANES, stride=CHUNK), :] for e in range(2)], axis=0
-        ).astype(BF16)
+    def store(t, side):
+        rows = pl.ds(pl.multiple_of(side * COLS + t * CHUNK, CHUNK), CHUNK)
+        return pltpu.make_async_copy(done.at[:, rows, :], out_ref.at[:, rows, :], sems.at[CHUNKS + side])
+
+    @pl.loop(0, CHUNKS)
+    def _(t):
+        pltpu.make_async_copy(pair_ref.at[:, pl.ds(t * CHUNK, CHUNK), :], held.at[t], sems.at[t]).wait()
+        group = 8
+        for n in range(ROWS // group):
+            block = held[t, n * group : (n + 1) * group].reshape(group * CHUNK, C).astype(F32)
+            normed[n * group * CHUNK : (n + 1) * group * CHUNK, :] = layer_norm(block, gain, bias, -1)
+        for n in range(CHUNK // 2):
+            x = jnp.concatenate(
+                [normed[pl.ds(2 * n + e, LANES, stride=CHUNK), :] for e in range(2)], axis=0
+            ).astype(BF16)
+            for side in range(2):
+                value = product(x, side)
+                for e in range(2):
+                    dense[side, pl.ds(2 * n + e, C, stride=CHUNK), :] = value[:, e * 128 : (e + 1) * 128]
+        for n in range(CHUNK // 8):
+            x = jnp.concatenate(
+                [normed[pl.ds(LANES * CHUNK + 8 * n + e, REST, stride=CHUNK), :] for e in range(8)], axis=0
+            ).astype(BF16)
+            for side in range(2):
+                value = product(x, side)
+                for e in range(2):
+                    at = side * TAIL + 4 * t + 2 * n + e
+                    tail[pl.ds(at, C, stride=2 * TAIL), :] = value[:, e * 128 : (e + 1) * 128]
         for side in range(2):
-            value = product(x, side)
-            for e in range(2):
-                dense[side, pl.ds(2 * n + e, C, stride=CHUNK), :] = value[:, e * 128 : (e + 1) * 128]
-
-    for n in range(2):
-        x = jnp.concatenate(
-            [
-                normed[pl.ds(LANES * CHUNK + 8 * n + e, REST, stride=CHUNK), :]
-                for e in range(8)
-            ],
-            axis=0,
-        ).astype(BF16)
+            to = pl.multiple_of(side * COLS + t * CHUNK, CHUNK)
+            for n in range(C // 8):
+                done[8 * n : 8 * n + 8, pl.ds(to, CHUNK), :] = (
+                    dense[side, n * 8 * CHUNK : (n + 1) * 8 * CHUNK, :].reshape(8, CHUNK, LANES).astype(BF16)
+                )
+            store(t, side).start()
+
+    for n in range(C // 8):
+        done[8 * n : 8 * n + 8, 2 * COLS :, :] = (
+            tail[n * 16 * TAIL : (n + 1) * 16 * TAIL, :].reshape(8, 2 * TAIL, LANES).astype(BF16)
+        )
+    rows = pl.ds(2 * COLS, 2 * TAIL)
+    last = pltpu.make_async_copy(done.at[:, rows, :], out_ref.at[:, rows, :], sems.at[CHUNKS + 2])
+    last.start()
+    last.wait()
+    for t in range(CHUNKS):
         for side in range(2):
-            value = product(x, side)
-            for e in range(2):
-                tail[pl.ds(side * TAIL + 4 * step + 2 * n + e, C, stride=2 * TAIL), :] = value[:, e * 128 : (e + 1) * 128]
-
-    @pl.loop(0, C // 8)
-    def _(n):
-        at = pl.multiple_of(n * 8 * CHUNK, 8 * CHUNK)
-        for side in range(2):
-            to = pl.multiple_of(side * COLS + step * CHUNK, CHUNK)
-            out_ref[pl.ds(8 * n, 8), pl.ds(to, CHUNK), :] = (
-                dense[side, pl.ds(at, 8 * CHUNK), :].reshape(8, CHUNK, LANES).astype(BF16)
-            )
-
-    @pl.when(step == COLS // CHUNK - 1)
-    def _():
-        @pl.loop(0, C // 8)
-        def _(n):
-            at = pl.multiple_of(n * 16 * TAIL, 16 * TAIL)
-            out_ref[pl.ds(8 * n, 8), 2 * COLS :, :] = (
-                tail[pl.ds(at, 16 * TAIL), :].reshape(8, 2 * TAIL, LANES).astype(BF16)
-            )
+            store(t, side).wait()
 
 
 def edges(pair, gain, bias, weight):
+    vmem = pl.BlockSpec(memory_space=pltpu.VMEM)
     return pl.pallas_call(
         edges_kernel,
-        grid=(COLS // CHUNK,),
-        in_specs=[
-            pl.BlockSpec((ROWS, CHUNK, C), lambda t: (0, t, 0)),
-            pl.BlockSpec((1, C), lambda t: (0, 0)),
-            pl.BlockSpec((1, C), lambda t: (0, 0)),
-            pl.BlockSpec((C, 4 * C), lambda t: (0, 0)),
-        ],
-        out_specs=pl.BlockSpec((C, BOTH, LANES), lambda t: (0, 0, 0)),
+        in_specs=[pl.BlockSpec(memory_space=pl.ANY), vmem, vmem, vmem],
+        out_specs=pl.BlockSpec(memory_space=pl.ANY),
         out_shape=jax.ShapeDtypeStruct((C, BOTH, LANES), BF16),
         scratch_shapes=[
             pltpu.VMEM((4 * C, C), BF16),
+            pltpu.VMEM((CHUNKS, ROWS, CHUNK, C), BF16),
             pltpu.VMEM((ROWS * CHUNK, C), F32),
             pltpu.VMEM((2, C * CHUNK, LANES), F32),
             pltpu.VMEM((C * 2 * TAIL, LANES), F32),
+            pltpu.VMEM((C, BOTH, LANES), BF16),
+            pltpu.SemaphoreType.DMA((CHUNKS + 3,)),
         ],
-        compiler_params=pltpu.CompilerParams(vmem_limit_bytes=40 * MIB),
+        compiler_params=pltpu.CompilerParams(vmem_limit_bytes=VMEM_BYTES),
         cost_estimate=pl.CostEstimate(flops=2 * ROWS * COLS * C * 4 * C, bytes_accessed=10 * MIB, transcendentals=0),
         name="edges",
     )(pair, gain[None, :], bias[None, :], weight)
@@ -229,84 +229,105 @@
             pltpu.VMEM((N_ROW * N_CHAN, BACK - COLS, LANES), BF16),
             pltpu.SemaphoreType.DMA((5,)),
         ],
-        compiler_params=pltpu.CompilerParams(vmem_limit_bytes=48 * MIB),
+        compiler_params=pltpu.CompilerParams(vmem_limit_bytes=VMEM_BYTES),
         cost_estimate=pl.CostEstimate(flops=2 * SIDE**3, bytes_accessed=10 * MIB, transcendentals=0),
         name="triangle",
     )(edges_all)
 
 
-def finish_kernel(tri_ref, gate_ref, gain_ref, bias_ref, weight_ref, out_ref, wide, dense, tail):
-    step = pl.program_id(0)
-    full = COLS // CHUNK
-    gain, bias, weight = gain_ref[...], bias_ref[...], weight_ref[...]
-
-    @pl.loop(0, C // 8)
-    def _(n):
-        at = pl.multiple_of(n * 8 * CHUNK, 8 * CHUNK)
-        wide[pl.ds(at, 8 * CHUNK), :] = tri_ref[pl.ds(8 * n, 8)].reshape(8 * CHUNK, LANES).astype(F32)
-
-    def project(g):
-        normed = layer_norm(wide[pl.ds(g, C, stride=CHUNK), :], gain, bias, 0).astype(BF16)
+def finish_kernel(
+    tri_ref, gate_ref, gain_ref, bias_ref, weight_ref, out_ref, held, held_gate, wide, dense, tail, done, sems
+):
+    span = BACK - COLS
+
+    def load(t):
+        rows = pl.ds(pl.multiple_of(t * CHUNK, CHUNK), CHUNK)
+        return (
+            pltpu.make_async_copy(tri_ref.at[:, rows, :], held.at[:, rows, :], sems.at[t]),
+            pltpu.make_async_copy(
+                gate_ref.at[pl.ds(0, LANES), rows, :], held_gate.at[pl.ds(0, LANES), rows, :], sems.at[CHUNKS + t]
+            ),
+        )
+
+    def store(t):
+        rows = pl.ds(pl.multiple_of(t * CHUNK, CHUNK), CHUNK)
+        return pltpu.make_async_copy(
+            done.at[pl.ds(0, LANES), rows, :], out_ref.at[pl.ds(0, LANES), rows, :], sems.at[2 * CHUNKS + 2]
+        )
+
+    rows, rest = pl.ds(COLS, span), pl.ds(LANES, REST)
+    tri_tail = pltpu.make_async_copy(tri_ref.at[:, rows, :], held.at[:, rows, :], sems.at[2 * CHUNKS])
+    gate_tail = pltpu.make_async_copy(gate_ref.at[rest], held_gate.at[rest], sems.at[2 * CHUNKS + 1])
+    tri_tail.start()
+    for t in range(CHUNKS):
+        for copy in load(t):
+            copy.start()
+    gate_tail.start()
+    gain = jnp.broadcast_to(gain_ref[...], (LANES, C)).T
+    bias = jnp.broadcast_to(bias_ref[...], (LANES, C)).T
+    weight = weight_ref[...]
+
+    def project(g, stride):
+        normed = layer_norm(wide[pl.ds(g, C, stride=stride), :], gain, bias, 0).astype(BF16)
         return lax.dot_general(normed, weight, (((0,), (0,)), ((), ())), preferred_element_type=F32)
 
-    @pl.when(step < full)
-    def _():
-        @pl.loop(0, CHUNK)
-        def _(g):
-            dense[pl.ds(g, LANES, stride=CHUNK), :] = project(g)
-
-        to = pl.multiple_of(step * CHUNK, CHUNK)
-
-        @pl.loop(0, LANES // 8)
-        def _(n):
-            at = pl.multiple_of(n * 8 * CHUNK, 8 * CHUNK)
-            value = dense[pl.ds(at, 8 * CHUNK), :].reshape(8, CHUNK, C)
-            gate = gate_ref[pl.ds(8 * n, 8), pl.ds(to, CHUNK), :].astype(F32)
-            out_ref[pl.ds(8 * n, 8), pl.ds(to, CHUNK), :] = (gate * value).astype(BF16)
-
-    @pl.when(step >= full)
-    def _():
-        first = (step - full) * CHUNK
-
-        @pl.loop(0, jnp.minimum(CHUNK, TAIL - first))
-        def _(g):
-            value = project(g)
-            for e in range(PACK):
-                tail[pl.ds(PACK * (first + g) + e, REST, stride=COLS), :] = value[e * REST : (e + 1) * REST]
-
-    @pl.when(step == pl.num_programs(0) - 1)
-    def _():
-        @pl.loop(0, REST // 8)
-        def _(n):
-            at = pl.multiple_of(n * 8 * COLS, 8 * COLS)
-            value = tail[pl.ds(at, 8 * COLS), :].reshape(8, COLS, C)
-            gate = gate_ref[pl.ds(LANES + 8 * n, 8)].astype(F32)
-            out_ref[pl.ds(LANES + 8 * n, 8)] = (gate * value).astype(BF16)
+    tri_tail.wait()
+    for n in range(C // 8):
+        wide[n * 8 * span : (n + 1) * 8 * span, :] = held[8 * n : 8 * n + 8, COLS:, :].reshape(8 * span, LANES).astype(F32)
+    for m in range(TAIL):
+        value = project(m, span)
+        for e in range(PACK):
+            tail[pl.ds(PACK * m + e, REST, stride=COLS), :] = value[e * REST : (e + 1) * REST]
+
+    @pl.loop(0, CHUNKS)
+    def _(t):
+        for copy in load(t):
+            copy.wait()
+        to = pl.multiple_of(t * CHUNK, CHUNK)
+        for n in range(C // 8):
+            wide[n * 8 * CHUNK : (n + 1) * 8 * CHUNK, :] = (
+                held[8 * n : 8 * n + 8, pl.ds(to, CHUNK), :].reshape(8 * CHUNK, LANES).astype(F32)
+            )
+        for g in range(CHUNK):
+            dense[pl.ds(g, LANES, stride=CHUNK), :] = project(g, CHUNK)
+        for n in range(LANES // 8):
+            value = dense[n * 8 * CHUNK : (n + 1) * 8 * CHUNK, :].reshape(8, CHUNK, C)
+            gate = held_gate[8 * n : 8 * n + 8, pl.ds(to, CHUNK), :].astype(F32)
+            done[8 * n : 8 * n + 8, pl.ds(to, CHUNK), :] = (gate * value).astype(BF16)
+        store(t).start()
+
+    gate_tail.wait()
+    for n in range(REST // 8):
+        value = tail[n * 8 * COLS : (n + 1) * 8 * COLS, :].reshape(8, COLS, C)
+        gate = held_gate[LANES + 8 * n : LANES + 8 * n + 8].astype(F32)
+        done[LANES + 8 * n : LANES + 8 * n + 8] = (gate * value).astype(BF16)
+    last = pltpu.make_async_copy(done.at[rest], out_ref.at[rest], sems.at[2 * CHUNKS + 3])
+    last.start()
+    last.wait()
+    for t in range(CHUNKS):
+        store(t).wait()
 
 
 def finish(tri, gate, gain, bias, weight):
-    steps = COLS // CHUNK + -(-TAIL // CHUNK)
+    vmem, hbm = pl.BlockSpec(memory_space=pltpu.VMEM), pl.BlockSpec(memory_space=pl.ANY)
     return pl.pallas_call(
         finish_kernel,
-        grid=(steps,),
-        in_specs=[
-            pl.BlockSpec((C, CHUNK, LANES), lambda t: (0, t, 0)),
-            pl.BlockSpec((ROWS, COLS, C), lambda t: (0, 0, 0)),
-            pl.BlockSpec((C, 1), lambda t: (0, 0)),
-            pl.BlockSpec((C, 1), lambda t: (0, 0)),
-            pl.BlockSpec((C, C), lambda t: (0, 0)),
-        ],
-        out_specs=pl.BlockSpec((ROWS, COLS, C), lambda t: (0, 0, 0)),
+        in_specs=[hbm, hbm, vmem, vmem, vmem],
+        out_specs=hbm,
         out_shape=jax.ShapeDtypeStruct((ROWS, COLS, C), BF16),
         scratch_shapes=[
-            pltpu.VMEM((C * CHUNK, LANES), F32),
+            pltpu.VMEM((C, BACK, LANES), BF16),
+            pltpu.VMEM((ROWS, COLS, C), BF16),
+            pltpu.VMEM((C * (BACK - COLS), LANES), F32),
             pltpu.VMEM((LANES * CHUNK, C), F32),
             pltpu.VMEM((REST * COLS, C), F32),
+            pltpu.VMEM((ROWS, COLS, C), BF16),
+            pltpu.SemaphoreType.DMA((2 * CHUNKS + 4,)),
         ],
-        compiler_params=pltpu.CompilerParams(vmem_limit_bytes=40 * MIB),
+        compiler_params=pltpu.CompilerParams(vmem_limit_bytes=VMEM_BYTES),
         cost_estimate=pl.CostEstimate(flops=2 * ROWS * COLS * C * C, bytes_accessed=10 * MIB, transcendentals=0),
         name="finish",
-    )(tri, gate, gain[:, None], bias[:, None], weight)
+    )(tri, gate, gain[None, :], bias[None, :], weight)
 
 
 def shards(pair, in_gain, in_bias, edge_weight, gate_weight, out_gain, out_bias, out_weight):

time: 232 us -> 178 us (0.77)
  Pallas kernels: 84.1 us -> 37.1 us
  local copies, waits for them, and re-layouts: 8.09 us -> 0.02 us
    pallas_call x2, Pallas kernels: 69 us -> 25.7 us  [the longest x1 15.2 us: edges(): pl.pallas_call(edges_kernel, in_specs=[pl.BlockSpec(memory_space=pl.ANY),...]
    unnamed x26 -> x8, local copies, waits for them, and re-layouts: 7.87 us -> 0.02 us
    pallas_call x1, Pallas kernels: 15.1 us -> 11.3 us  [triangle(): pl.pallas_call(triangle_kernel, in_specs=[pl.BlockSpec(memory_space=pl.AN...]
  transfers between devices with their start and end apart: 1 -> 1, of which waited for: 1 -> 1; matrix products, arithmetic and copies ran while one was open for 6% -> 8% of each run, Pallas kernels for 0% -> 0%
where the time goes in v2:
time: 178 us
  blocking collectives  91 us (51%)
  Pallas kernels  37.1 us (21%)
  waiting for transfers between devices  30.3 us (17%)
  matrix products  7.14 us (4%)
  other arithmetic  6.41 us (4%)
  starting transfers between devices  5.44 us (3%)
    all_to_all x1, blocking collectives, shards(): lax.all_to_all(both, ('row', 'chan'), split_axis=0, concat_axis=0, tiled=...  91 us
    all_to_all x1, waiting for transfers between devices, shards(): lax.all_to_all(triangle(both_all), ('row', 'chan'), split_axis=0, concat_...  30.3 us
    pallas_call x1, Pallas kernels, edges(): pl.pallas_call(edges_kernel, in_specs=[pl.BlockSpec(memory_space=pl.ANY),...  15.2 us
    pallas_call x1, Pallas kernels, triangle(): pl.pallas_call(triangle_kernel, in_specs=[pl.BlockSpec(memory_space=pl.AN...  11.3 us
    pallas_call x1, Pallas kernels, finish(): pl.pallas_call(finish_kernel, in_specs=[hbm, hbm, vmem, vmem, vmem], out_...  10.5 us
    dot_general x1, matrix products, shards(): jnp.einsum('pqc,cd->pqd', normed, gate_weight, preferred_element_type=F32)  7.14 us
    all_to_all x1, starting transfers between devices, shards(): lax.all_to_all(triangle(both_all), ('row', 'chan'), split_axis=0, concat_...  5.44 us
    reduce_sum x1, other arithmetic, layer_norm(): var = jnp.mean(centred * centred, axis=axis, keepdims=True)  4.9 us
  transfers between devices with their start and end apart: 1, of which 1 were waited for; matrix products, arithmetic and copies ran while one was open for 8% of the time, Pallas kernels for 0%

profile of v2, /device:TPU:1, one launch (start us, length us, event | category | flops | bytes accessed | tf_op | source)
XLA Modules:
  0.0 177.7 jit_solution(6095162708543579684)
XLA Ops:
  0.0 0.0 copy-start
  0.0 15.2 %edges.1 = bf16[128,200,128]{2,1,0:T(8,128)(2,1)} custom-call(bf16[160,80,128]{2,1,0:T(8,128)(2,1)} %pair_ref.1, f32[1,128]{1,0:T(1,128)} %bitcast.7, f32[1,128]{1,0:T(1,128)} %bitcast.8, bf16[128,512]{1,0:T(8,128)(2,1)} %weight_ref.2), custom_call_target="tpu_custom_call" | custom-call | flops 1677721600 | bytes 10485760 | tf_op jit(solution)/shard_map/edges/pallas_call | solution.py:102
  15.2 91.0 %all_to_all.10.edges_ref = bf16[128,200,128]{2,1,0:T(8,128)(2,1)} all-to-all(bf16[128,200,128]{2,1,0:T(8,128)(2,1)} %edges.1), channel_id=1, replica_groups=mesh['chan'=16,'row'=8] {'row','chan'}, dimensions={0} | all-to-all | bytes 13107200 | tf_op jit(solution)/shard_map/all_to_all | solution.py:335
  106.2 11.3 %triangle.1 = bf16[128,104,128]{2,1,0:T(8,128)(2,1)} custom-call(bf16[128,200,128]{2,1,0:T(8,128)(2,1)} %all_to_all.10.edges_ref), custom_call_target="tpu_custom_call" | custom-call | flops 4194304000 | bytes 10485760 | tf_op jit(solution)/shard_map/triangle/pallas_call | solution.py:215
  117.6 0.0 copy-start.1
  117.6 0.0 copy-start.2
  117.6 0.0 copy-start.3
  117.6 5.4 %all-to-all-start.1 = ((bf16[128,104,128]{2,1,0:T(8,128)(2,1)}), bf16[128,104,128]{2,1,0:T(8,128)(2,1)}, u32[]{:S(2)}, u32[]{:S(2)}) async-start(bf16[128,104,128]{2,1,0:T(8,128)(2,1)} %triangle.1), calls=%async_computation.1 | async-start | bytes 6815744 | tf_op jit(solution)/shard_map/all_to_all | solution.py:340
  123.0 0.0 copy-done.1
  123.1 1.5 convert_reduce_fusion
  124.5 4.9 %fusion.2 = f32[160,80]{1,0:T(8,128)S(1)} fusion(bf16[160,80,128]{2,1,0:T(8,128)(2,1)S(1)} %copy-done.1, f32[160,80]{1,0:T(8,128)S(1)} %broadcast_multiply_fusion), kind=kLoop, calls=%fused_computation.4 | loop fusion | flops 6540800 | bytes 3379200 | tf_op jit(solution)/shard_map/reduce_sum | solution.py:31
  129.5 0.0 copy-done
  129.5 0.0 copy-done.2
  129.5 0.0 copy-done.3
  129.5 7.1 %divide_convert_fusion.gate_ref = bf16[160,80,128]{2,1,0:T(8,128)(2,1)} fusion(bf16[160,80,128]{2,1,0:T(8,128)(2,1)S(1)} %copy-done.1, f32[128]{0:T(128)S(1)} %copy-done.3, f32[128]{0:T(128)S(1)} %copy-done.2, f32[160,80]{1,0:T(8,128)S(1)} %add_rsqrt_fusion, f32[160,80]{1,0:T(8,128)S(1)} %broadcast_multiply_fusion, bf16[128,128]{1,0:T(8,128)(2,1)S(1)} %copy-done), kind=kOutput, calls=%fused_computation.8 | convolution fusion | flops 435814400 | bytes 6689792 | tf_op jit(solution)/shard_map/pqc,cd->pqd/dot_general | solution.py:338
  136.7 30.3 %all-to-all-done.1.tri_ref = bf16[128,104,128]{2,1,0:T(8,128)(2,1)} async-done(((bf16[128,104,128]{2,1,0:T(8,128)(2,1)}), bf16[128,104,128]{2,1,0:T(8,128)(2,1)}, u32[]{:S(2)}, u32[]{:S(2)}) %all-to-all-start.1) | async-done | bytes 3407904 | tf_op jit(solution)/shard_map/all_to_all | solution.py:340
  167.0 10.5 %finish.1 = bf16[160,80,128]{2,1,0:T(8,128)(2,1)} custom-call(bf16[128,104,128]{2,1,0:T(8,128)(2,1)} %all-to-all-done.1.tri_ref, bf16[160,80,128]{2,1,0:T(8,128)(2,1)} %divide_convert_fusion.gate_ref, f32[1,128]{1,0:T(1,128)} %bitcast.9, f32[1,128]{1,0:T(1,128)} %bitcast.10, bf16[128,128]{1,0:T(8,128)(2,1)} %weight_ref.3), custom_call_target="tpu_custom_call" | custom-call | flops 419430400 | bytes 10485760 | tf_op jit(solution)/shard_map/finish/pallas_call | solution.py:313
  (2 shorter events, 0.0 us)
Async XLA Ops:
  0.0 129.5 %copy-start = (bf16[128,128]{1,0:T(8,128)(2,1)S(1)}, bf16[128,128]{1,0:T(8,128)(2,1)}, u32[]{:S(2)}) copy-start(bf16[128,128]{1,0:T(8,128)(2,1)} %param.12) | copy-start | bytes 98308
  117.6 5.5 %copy-start.1 = (bf16[160,80,128]{2,1,0:T(8,128)(2,1)S(1)}, bf16[160,80,128]{2,1,0:T(8,128)(2,1)}, u32[]{:S(2)}) copy-start(bf16[160,80,128]{2,1,0:T(8,128)(2,1)} %pair_ref.1) | copy-start | bytes 9830404
  117.6 11.9 %copy-start.2 = (f32[128]{0:T(128)S(1)}, f32[128]{0:T(128)}, u32[]{:S(2)}) copy-start(f32[128]{0:T(128)} %param.9) | copy-start | bytes 1540
  117.6 11.9 %copy-start.3 = (f32[128]{0:T(128)S(1)}, f32[128]{0:T(128)}, u32[]{:S(2)}) copy-start(f32[128]{0:T(128)} %param.10) | copy-start | bytes 1540
  117.6 49.4 %all-to-all-start.1 = ((bf16[128,104,128]{2,1,0:T(8,128)(2,1)}), bf16[128,104,128]{2,1,0:T(8,128)(2,1)}, u32[]{:S(2)}, u32[]{:S(2)}) async-start(bf16[128,104,128]{2,1,0:T(8,128)(2,1)} %triangle.1), calls=%async_computation.1 | async-start | bytes 6815744 | tf_op jit(solution)/shard_map/all_to_all | solution.py:340

commit v3 on v0

v3 whole, which is shorter than its diff:
```python
import jax
import jax.numpy as jnp
from jax import lax
from jax.experimental import pallas as pl
from jax.experimental.pallas import tpu as pltpu
from jax.sharding import Mesh, PartitionSpec as P

ROWS, COLS, C = 160, 80, 128
LANES = 128
REST = ROWS - LANES
PACK = LANES // REST
TAIL = COLS // PACK
CHUNK = 16
CHUNKS = COLS // CHUNK
STEP = CHUNK + 4
TAIL_STEP = 2 * TAIL + 4
COLS_STEP = COLS + 4
BOTH = 2 * (COLS + TAIL)
BACK = 104
N_ROW, N_CHAN = 8, 16
SIZES = {"y": 4, "z_lo": 2, "core": 2, "z_hi": 2, "x": 4}
ROW, CHAN = ("z_hi", "x"), ("y", "z_lo", "core")
OUT_ORDER = ROW + CHAN
BACK_ORDER = ("y", "x", "core", "z_lo", "z_hi")
SIDE = 1280
F32, BF16 = jnp.float32, jnp.bfloat16
MIB = 1 << 20
VMEM_BYTES = 36 * MIB


def places(order, inside):
    found = []
    for n in range(N_ROW * N_CHAN):
        at = {}
        for axis in reversed(inside):
            n, at[axis] = divmod(n, SIZES[axis])
        number = 0
        for axis in order:
            number = number * SIZES[axis] + at[axis]
        found.append(number)
    return found


OUT_OF_CHANNEL = places(OUT_ORDER, BACK_ORDER)
FROM_BLOCK = places(OUT_ORDER, ROW + CHAN)
BACK_TO_BLOCK = places(BACK_ORDER, ROW + CHAN)


def layer_norm(values, gain, bias, axis):
    mean = jnp.mean(values, axis=axis, keepdims=True)
    centred = values - mean
    var = jnp.mean(centred * centred, axis=axis, keepdims=True)
    return centred * lax.rsqrt(var + 1e-05) * gain + bias


def fetch(sources, targets, sems):
    copies = [pltpu.make_async_copy(src, dst, sems.at[n]) for n, (src, dst) in enumerate(zip(sources, targets))]
    for copy in copies:
        copy.start()
    return copies


def edges_kernel(
    pair_ref, gain_hbm, bias_hbm, weight_hbm, out_ref, gain_ref, bias_ref, weight_ref, weight_t, held, normed, dense,
    tail, sems, small_sems
):
    loads = [
        pltpu.make_async_copy(pair_ref.at[:, pl.ds(t * CHUNK, CHUNK), :], held.at[t], sems.at[t]) for t in range(CHUNKS)
    ]
    for load in loads:
        load.start()
    small = (gain_ref, bias_ref, weight_ref)
    for copy in fetch((gain_hbm, bias_hbm, weight_hbm), small, small_sems):
        copy.wait()
    for m in range(4):
        turned = (0.5 * weight_ref[:, m * C : (m + 1) * C].astype(F32)).T.astype(BF16)
        for b in range(C // 16):
            at = 2 * C * (m // 2) + 32 * b + 16 * (m % 2)
            weight_t[at : at + 16, :] = turned[16 * b : 16 * b + 16]
    gain, bias = gain_ref[...], bias_ref[...]

    def product(x, side):
        both = lax.dot_general(
            weight_t[side * 2 * C : (side + 1) * 2 * C, :], x, (((1,), (1,)), ((), ())), preferred_element_type=F32
        )
        both = both.reshape(C // 16, 2, 16, x.shape[0])
        return (both[:, 0] * jnp.tanh(both[:, 1]) + both[:, 0]).reshape(C, x.shape[0])

    @pl.loop(0, CHUNKS)
    def _(t):
        pltpu.make_async_copy(pair_ref.at[:, pl.ds(t * CHUNK, CHUNK), :], held.at[t], sems.at[t]).wait()
        group = 8
        for n in range(ROWS // group):
            block = held[t, n * group : (n + 1) * group].reshape(group * CHUNK, C).astype(F32)
            block = layer_norm(block, gain, bias, -1)
            for u in range(group):
                at = (n * group + u) * STEP
                normed[at : at + CHUNK, :] = block[u * CHUNK : (u + 1) * CHUNK]
        for n in range(CHUNK // 2):
            x = jnp.concatenate(
                [normed[pl.ds(2 * n + e, LANES, stride=STEP), :] for e in range(2)], axis=0
            ).astype(BF16)
            for side in range(2):
                value = product(x, side)
                for e in range(2):
                    dense[side, pl.ds(2 * n + e, C, stride=STEP), :] = value[:, e * 128 : (e + 1) * 128]
        for n in range(CHUNK // 8):
            x = jnp.concatenate(
                [normed[pl.ds(LANES * STEP + 8 * n + e, REST, stride=STEP), :] for e in range(8)], axis=0
            ).astype(BF16)
            for side in range(2):
                value = product(x, side)
                for e in range(2):
                    at = side * TAIL + 4 * t + 2 * n + e
                    tail[pl.ds(at, C, stride=TAIL_STEP), :] = value[:, e * 128 : (e + 1) * 128]
        for side in range(2):
            to = pl.multiple_of(side * COLS + t * CHUNK, CHUNK)
            for h in range(C):
                out_ref[OUT_OF_CHANNEL[h], pl.ds(to, CHUNK), :] = dense[side, h * STEP : h * STEP + CHUNK, :].astype(BF16)

    for h in range(C):
        out_ref[OUT_OF_CHANNEL[h], 2 * COLS :, :] = tail[h * TAIL_STEP : h * TAIL_STEP + 2 * TAIL, :].astype(BF16)


def edges(pair, gain, bias, weight):
    vmem, hbm = pl.BlockSpec(memory_space=pltpu.VMEM), pl.BlockSpec(memory_space=pltpu.HBM)
    return pl.pallas_call(
        edges_kernel,
        in_specs=[hbm] * 4,
        out_specs=vmem,
        out_shape=jax.ShapeDtypeStruct((C, BOTH, LANES), BF16),
        scratch_shapes=[
            pltpu.VMEM((1, C), F32),
            pltpu.VMEM((1, C), F32),
            pltpu.VMEM((C, 4 * C), BF16),
            pltpu.VMEM((4 * C, C), BF16),
            pltpu.VMEM((CHUNKS, ROWS, CHUNK, C), BF16),
            pltpu.VMEM((ROWS * STEP, C), F32),
            pltpu.VMEM((2, C * STEP, LANES), F32),
            pltpu.VMEM((C * TAIL_STEP, LANES), F32),
            pltpu.SemaphoreType.DMA((CHUNKS,)),
            pltpu.SemaphoreType.DMA((3,)),
        ],
        compiler_params=pltpu.CompilerParams(vmem_limit_bytes=VMEM_BYTES),
        cost_estimate=pl.CostEstimate(flops=2 * ROWS * COLS * C * 4 * C, bytes_accessed=10 * MIB, transcendentals=0),
        name="edges",
    )(pair, gain[None, :], bias[None, :], weight)


def gate_kernel(
    pair_ref, gain_hbm, bias_hbm, weight_hbm, out_ref, gain_ref, bias_ref, weight_ref, held, sems
):
    for copy in fetch((pair_ref, gain_hbm, bias_hbm, weight_hbm), (held, gain_ref, bias_ref, weight_ref), sems):
        copy.wait()
    gain, bias, weight = gain_ref[...], bias_ref[...], weight_ref[...]
    group = 4

    @pl.loop(0, ROWS // group, unroll=2)
    def _(n):
        block = held[pl.ds(n * group, group)].reshape(group * COLS, C).astype(F32)
        normed = layer_norm(block, gain, bias, -1).astype(BF16)
        value = jax.nn.sigmoid(jnp.dot(normed, weight, preferred_element_type=F32))
        out_ref[pl.ds(n * group, group)] = value.astype(BF16).reshape(group, COLS, C)


def gates(pair, gain, bias, weight):
    vmem, hbm = pl.BlockSpec(memory_space=pltpu.VMEM), pl.BlockSpec(memory_space=pltpu.HBM)
    return pl.pallas_call(
        gate_kernel,
        in_specs=[hbm] * 4,
        out_specs=vmem,
        out_shape=jax.ShapeDtypeStruct((ROWS, COLS, C), BF16),
        scratch_shapes=[
            pltpu.VMEM((1, C), F32),
            pltpu.VMEM((1, C), F32),
            pltpu.VMEM((C, C), BF16),
            pltpu.VMEM((ROWS, COLS, C), BF16),
            pltpu.SemaphoreType.DMA((4,)),
        ],
        compiler_params=pltpu.CompilerParams(vmem_limit_bytes=VMEM_BYTES),
        cost_estimate=pl.CostEstimate(flops=2 * ROWS * COLS * C * C, bytes_accessed=30 * MIB, transcendentals=0),
        name="gates",
    )(pair, gain[None, :], bias[None, :], weight)


def regroup(pieces, lane):
    out = []
    for b in range(PACK):
        total = None
        for a in range(PACK):
            shift = ((a - b) * REST) % LANES
            moved = pltpu.roll(pieces[a], shift, 1) if shift else pieces[a]
            total = moved if total is None else jnp.where(lane // REST == a, moved, total)
        out.append(total)
    return out


def triangle_kernel(edges_ref, out_ref, left_rest, right_t, rest_left, rest_right, tri_rest):
    lane = lax.broadcasted_iota(jnp.int32, (2 * TAIL, LANES), 1)
    for c in range(N_CHAN):
        for q in range(N_ROW // PACK):
            blocks = [FROM_BLOCK[(q * PACK + a) * N_CHAN + c] for a in range(PACK)]
            pieces = [edges_ref[block, 2 * COLS :, :].astype(F32) for block in blocks]
            for b, value in enumerate(regroup(pieces, lane)):
                rest_left[q, pl.ds(c * COLS + b, TAIL, stride=PACK), :] = value[:TAIL]
                rest_right[q, pl.ds(c * COLS + b, TAIL, stride=PACK), :] = value[TAIL:]

    def side(r, first):
        blocks = FROM_BLOCK[r * N_CHAN : (r + 1) * N_CHAN]
        return jnp.concatenate([edges_ref[block, first : first + COLS, :] for block in blocks], axis=0)

    for q in range(N_ROW // PACK):
        left_rest[:, q * LANES : (q + 1) * LANES] = rest_left[q].astype(BF16)
        turned = rest_right[q].astype(BF16).T
        for a in range(PACK):
            at = (q * PACK + a) * ROWS + LANES
            right_t[at : at + REST, :] = turned[a * REST : (a + 1) * REST]
    for r in range(N_ROW):
        right_t[r * ROWS : r * ROWS + LANES, :] = side(r, COLS).T

    part = jnp.dot(right_t[...], left_rest[...], preferred_element_type=F32)
    for q in range(N_ROW // PACK):
        tri_rest[q] = part[:, q * LANES : (q + 1) * LANES]
    lane = lax.broadcasted_iota(jnp.int32, (TAIL, LANES), 1)
    for n in range(N_ROW // 2):
        for c in range(4 * n, 4 * n + 4):
            for q in range(N_ROW // PACK):
                pieces = [tri_rest[q, pl.ds(c * COLS + b, TAIL, stride=PACK), :] for b in range(PACK)]
                for a, value in enumerate(regroup(pieces, lane)):
                    value = jnp.concatenate([value, jnp.zeros((BACK - COLS - TAIL, LANES), F32)], axis=0)
                    out_ref[BACK_TO_BLOCK[(q * PACK + a) * N_CHAN + c], COLS:, :] = value.astype(BF16)
        pair = jnp.concatenate([side(2 * n, 0), side(2 * n + 1, 0)], axis=1)
        part = jnp.dot(right_t[...], pair, preferred_element_type=F32).astype(BF16)
        for e in range(2):
            r = 2 * n + e
            for c in range(N_CHAN):
                out_ref[BACK_TO_BLOCK[r * N_CHAN + c], :COLS, :] = part[
                    c * COLS : (c + 1) * COLS, e * LANES : (e + 1) * LANES
                ]


def triangle(edges_all):
    vmem = pl.BlockSpec(memory_space=pltpu.VMEM)
    return pl.pallas_call(
        triangle_kernel,
        in_specs=[vmem],
        out_specs=vmem,
        out_shape=jax.ShapeDtypeStruct((N_ROW * N_CHAN, BACK, LANES), BF16),
        scratch_shapes=[
            pltpu.VMEM((SIDE, 2 * LANES), BF16),
            pltpu.VMEM((SIDE, SIDE), BF16),
            pltpu.VMEM((N_ROW // PACK, SIDE, LANES), F32),
            pltpu.VMEM((N_ROW // PACK, SIDE, LANES), F32),
            pltpu.VMEM((N_ROW // PACK, SIDE, LANES), F32),
        ],
        compiler_params=pltpu.CompilerParams(vmem_limit_bytes=VMEM_BYTES),
        cost_estimate=pl.CostEstimate(flops=2 * SIDE**3, bytes_accessed=10 * MIB, transcendentals=0),
        name="triangle",
    )(edges_all)


def finish_kernel(
    held, gate_ref, gain_hbm, bias_hbm, weight_hbm, out_ref, gain_ref, bias_ref, weight_ref, wide, dense, tail, done,
    sems, small_sems
):
    def store(t):
        rows = pl.ds(pl.multiple_of(t * CHUNK, CHUNK), CHUNK)
        return pltpu.make_async_copy(
            done.at[pl.ds(0, LANES), rows, :], out_ref.at[pl.ds(0, LANES), rows, :], sems.at[0]
        )

    rest = pl.ds(LANES, REST)
    small = (gain_ref, bias_ref, weight_ref)
    for copy in fetch((gain_hbm, bias_hbm, weight_hbm), small, small_sems):
        copy.wait()
    gain = jnp.broadcast_to(gain_ref[...], (LANES, C)).T
    bias = jnp.broadcast_to(bias_ref[...], (LANES, C)).T
    weight = weight_ref[...]

    def project(g):
        normed = layer_norm(wide[pl.ds(g, C, stride=STEP), :], gain, bias, 0).astype(BF16)
        return lax.dot_general(normed, weight, (((0,), (0,)), ((), ())), preferred_element_type=F32)

    for h in range(C):
        wide[h * STEP : h * STEP + TAIL, :] = held[h, COLS:, :].astype(F32)[:TAIL]
    for m in range(TAIL):
        value = project(m)
        for e in range(PACK):
            tail[pl.ds(PACK * m + e, REST, stride=COLS_STEP), :] = value[e * REST : (e + 1) * REST]

    @pl.loop(0, CHUNKS)
    def _(t):
        to = pl.multiple_of(t * CHUNK, CHUNK)
        for h in range(C):
            wide[h * STEP : h * STEP + CHUNK, :] = held[h, pl.ds(to, CHUNK), :].astype(F32)
        for g in range(CHUNK):
            dense[pl.ds(g, LANES, stride=STEP), :] = project(g)
        for i in range(LANES):
            gate = gate_ref[i, pl.ds(to, CHUNK), :].astype(F32)
            done[i, pl.ds(to, CHUNK), :] = (gate * dense[i * STEP : i * STEP + CHUNK, :]).astype(BF16)
        store(t).start()

    for i in range(REST):
        gate = gate_ref[LANES + i].astype(F32)
        done[LANES + i] = (gate * tail[i * COLS_STEP : i * COLS_STEP + COLS, :]).astype(BF16)
    last = pltpu.make_async_copy(done.at[rest], out_ref.at[rest], sems.at[1])
    last.start()
    last.wait()
    for t in range(CHUNKS):
        store(t).wait()


def finish(tri, gate, gain, bias, weight):
    vmem, hbm = pl.BlockSpec(memory_space=pltpu.VMEM), pl.BlockSpec(memory_space=pltpu.HBM)
    return pl.pallas_call(
        finish_kernel,
        in_specs=[vmem, vmem, hbm, hbm, hbm],
        out_specs=hbm,
        out_shape=jax.ShapeDtypeStruct((ROWS, COLS, C), BF16),
        scratch_shapes=[
            pltpu.VMEM((1, C), F32),
            pltpu.VMEM((1, C), F32),
            pltpu.VMEM((C, C), BF16),
            pltpu.VMEM((C * STEP, LANES), F32),
            pltpu.VMEM((LANES * STEP, C), F32),
            pltpu.VMEM((REST * COLS_STEP, C), F32),
            pltpu.VMEM((ROWS, COLS, C), BF16),
            pltpu.SemaphoreType.DMA((2,)),
            pltpu.SemaphoreType.DMA((3,)),
        ],
        compiler_params=pltpu.CompilerParams(vmem_limit_bytes=VMEM_BYTES),
        cost_estimate=pl.CostEstimate(flops=2 * ROWS * COLS * C * C, bytes_accessed=10 * MIB, transcendentals=0),
        name="finish",
    )(tri, gate, gain[None, :], bias[None, :], weight)


def shards(pair, in_gain, in_bias, edge_weight, gate_weight, out_gain, out_bias, out_weight):
    both = edges(pair, in_gain, in_bias, edge_weight)
    both_all = lax.all_to_all(both, OUT_ORDER, split_axis=0, concat_axis=0, tiled=True)
    gate = gates(pair, in_gain, in_bias, gate_weight)
    tri = lax.all_to_all(triangle(both_all), BACK_ORDER, split_axis=0, concat_axis=0, tiled=True)
    return finish(tri, gate, out_gain, out_bias, out_weight)


def solution(mesh):
    apart = Mesh(mesh.devices.reshape(tuple(SIZES.values())), tuple(SIZES))
    return jax.shard_map(
        shards,
        mesh=apart,
        in_specs=(P(ROW, CHAN, None), P(), P(), P(), P(), P(), P(), P()),
        out_specs=P(ROW, CHAN, None),
        check_vma=False,
    )
```

time: 577 us -> 166 us (0.29)
  waiting for transfers between devices: 217 us -> 31.1 us
  blocking collectives: 212 us -> 90.7 us
  local copies, waits for them, and re-layouts: 63.9 us -> 11.4 us
  matrix products: 49 us -> 0 us
  Pallas kernels: 0 us -> 27.3 us
  other arithmetic: 20.1 us -> 0 us
  between operations: 13.5 us -> 0.1 us
    all_gather x1 -> x0, waiting for transfers between devices: 217 us -> none  [shards(): lax.all_gather(right_group, 'row', axis=1, tiled=True)]
    all_to_all x3 -> x1, blocking collectives: 212 us -> 90.7 us  [shards(): lax.all_to_all(both, OUT_ORDER, split_axis=0, concat_axis=0, tiled=True)]
    dot_general x7 -> x0, matrix products: 49 us -> none  [the longest x4 22.4 us: project(): jnp.einsum('pqc,ch->hpq', normed, edge_weight[:, index * width:(index + 1...]
    convert_element_type x4 -> x0, local copies, waits for them, and re-layouts: 33.4 us -> none  [the longest x1 9.76 us: shards(): tri_block.astype(jnp.float32)]
    all_to_all x0 -> x1, waiting for transfers between devices: none -> 31.1 us  [shards(): lax.all_to_all(triangle(both_all), BACK_ORDER, split_axis=0, concat_axis=...]
    all_to_all x4 -> x0, local copies, waits for them, and re-layouts: 28.4 us -> none  [the longest x2 14.8 us: shards(): lax.all_to_all(right, 'chan', split_axis=0, concat_axis=2, tiled=True)]
    pallas_call x0 -> x4, Pallas kernels: none -> 27.3 us  [the longest x1 8.19 us: gates(): pl.pallas_call(gate_kernel, in_specs=[hbm] * 4, out_specs=vmem, out_shape...]
    reduce_sum x4 -> x0, other arithmetic: 15.8 us -> none  [the longest x2 8.44 us: layer_norm(): mean = jnp.mean(values, axis=axis, keepdims=True)]
  transfers between devices with their start and end apart: 1 -> 1, of which waited for: 1 -> 1; matrix products, arithmetic and copies ran while one was open for 4% -> 0% of each run, Pallas kernels for 0% -> 5%
where the time goes in v3:
time: 166 us
  blocking collectives  90.7 us (55%)
  waiting for transfers between devices  31.1 us (19%)
  Pallas kernels  27.3 us (16%)
  local copies, waits for them, and re-layouts  11.4 us (7%)
  starting transfers between devices  5.03 us (3%)
    all_to_all x1, blocking collectives, shards(): lax.all_to_all(both, OUT_ORDER, split_axis=0, concat_axis=0, tiled=True)  90.7 us
    all_to_all x1, waiting for transfers between devices, shards(): lax.all_to_all(triangle(both_all), BACK_ORDER, split_axis=0, concat_axis=...  31.1 us
    unnamed x28, local copies, waits for them, and re-layouts  11.4 us
    pallas_call x1, Pallas kernels, gates(): pl.pallas_call(gate_kernel, in_specs=[hbm] * 4, out_specs=vmem, out_shape...  8.19 us
    pallas_call x1, Pallas kernels, edges(): pl.pallas_call(edges_kernel, in_specs=[hbm] * 4, out_specs=vmem, out_shap...  7.82 us
    pallas_call x1, Pallas kernels, triangle(): pl.pallas_call(triangle_kernel, in_specs=[vmem], out_specs=vmem, out_shap...  5.84 us
    pallas_call x1, Pallas kernels, finish(): pl.pallas_call(finish_kernel, in_specs=[vmem, vmem, hbm, hbm, hbm], out_s...  5.45 us
    all_to_all x1, starting transfers between devices, shards(): lax.all_to_all(triangle(both_all), BACK_ORDER, split_axis=0, concat_axis=...  5.03 us
  transfers between devices with their start and end apart: 1, of which 1 were waited for; matrix products, arithmetic and copies ran while one was open for 0% of the time, Pallas kernels for 5%

profile of v3, /device:TPU:1, one launch (start us, length us, event | category | flops | bytes accessed | tf_op | source)
XLA Modules:
  0.0 165.6 jit_solution(5212890740987605374)
XLA Ops:
  0.0 1.9 %copy-done = bf16[160,80,128]{2,1,0:T(8,128)(2,1)S(1)} copy-done((bf16[160,80,128]{2,1,0:T(8,128)(2,1)S(1)}, bf16[160,80,128]{2,1,0:T(8,128)(2,1)}, u32[]{:S(2)}) %copy-start) | copy-done | bytes 3276824
  1.9 0.9 copy-done.5
  2.8 0.7 copy-done.8
  3.5 0.7 copy-done.10
  4.1 7.8 %edges.1 = bf16[128,200,128]{2,1,0:T(8,128)(2,1)S(1)} custom-call(bf16[160,80,128]{2,1,0:T(8,128)(2,1)S(1)} %copy-done, f32[1,128]{1,0:T(1,128)S(1)} %bitcast.4, f32[1,128]{1,0:T(1,128)S(1)} %bitcast.6, bf16[128,512]{1,0:T(8,128)(2,1)S(1)} %copy-done.5), custom_call_target="tpu_custom_call" | custom-call | flops 1677721600 | bytes 10485760 | tf_op jit(solution)/shard_map/edges/pallas_call | solution.py:127
  12.0 90.7 %all_to_all.10.edges_ref = bf16[128,200,128]{2,1,0:T(8,128)(2,1)S(1)} all-to-all(bf16[128,200,128]{2,1,0:T(8,128)(2,1)S(1)} %edges.1), channel_id=1, replica_groups=mesh['y'=4,'z_lo'=2,'core'=2,'z_hi'=2,'x'=4] {'z_hi','x','y','z_lo','core'}, dimensions={0} | all-to-all | bytes 13107200 | tf_op jit(solution)/shard_map/all_to_all | solution.py:339
  102.6 5.8 %triangle.1 = bf16[128,104,128]{2,1,0:T(8,128)(2,1)S(1)} custom-call(bf16[128,200,128]{2,1,0:T(8,128)(2,1)S(1)} %all_to_all.10.edges_ref), custom_call_target="tpu_custom_call" | custom-call | flops 4194304000 | bytes 10485760 | tf_op jit(solution)/shard_map/triangle/pallas_call | solution.py:244
  108.5 0.0 copy-start.4
  108.5 1.7 %copy-done.4 = bf16[128,104,128]{2,1,0:T(8,128)(2,1)} copy-done((bf16[128,104,128]{2,1,0:T(8,128)(2,1)}, bf16[128,104,128]{2,1,0:T(8,128)(2,1)S(1)}, u32[]{:S(2)}) %copy-start.4) | copy-done | bytes 3407896
  110.2 5.0 %all-to-all-start.1 = ((bf16[128,104,128]{2,1,0:T(8,128)(2,1)}), bf16[128,104,128]{2,1,0:T(8,128)(2,1)S(1)}, u32[]{:S(2)}, u32[]{:S(2)}) async-start(bf16[128,104,128]{2,1,0:T(8,128)(2,1)} %copy-done.4), calls=%async_computation.1 | async-start | bytes 6815744 | tf_op jit(solution)/shard_map/all_to_all | solution.py:341
  115.2 0.0 copy-done.6
  115.3 0.0 copy-done.9
  115.3 0.0 copy-done.11
  115.3 0.0 copy-start.1
  115.3 1.9 %copy-done.1 = bf16[160,80,128]{2,1,0:T(8,128)(2,1)S(1)} copy-done((bf16[160,80,128]{2,1,0:T(8,128)(2,1)S(1)}, bf16[160,80,128]{2,1,0:T(8,128)(2,1)}, u32[]{:S(2)}) %copy-start.1) | copy-done | bytes 3276824
  117.2 8.2 %gates.1.gate_ref = bf16[160,80,128]{2,1,0:T(8,128)(2,1)S(1)} custom-call(bf16[160,80,128]{2,1,0:T(8,128)(2,1)S(1)} %copy-done.1, f32[1,128]{1,0:T(1,128)S(1)} %bitcast.5, f32[1,128]{1,0:T(1,128)S(1)} %bitcast.7, bf16[128,128]{1,0:T(8,128)(2,1)S(1)} %copy-done.6), custom_call_target="tpu_custom_call" | custom-call | flops 419430400 | bytes 31457280 | tf_op jit(solution)/shard_map/gates/pallas_call | solution.py:168
  125.4 0.0 copy-start.2
  125.4 1.7 %copy-done.2 = bf16[160,80,128]{2,1,0:T(8,128)(2,1)} copy-done((bf16[160,80,128]{2,1,0:T(8,128)(2,1)}, bf16[160,80,128]{2,1,0:T(8,128)(2,1)S(1)}, u32[]{:S(2)}) %copy-start.2) | copy-done | bytes 3276824
  127.1 31.1 %all-to-all-done.1.held = bf16[128,104,128]{2,1,0:T(8,128)(2,1)S(1)} async-done(((bf16[128,104,128]{2,1,0:T(8,128)(2,1)}), bf16[128,104,128]{2,1,0:T(8,128)(2,1)S(1)}, u32[]{:S(2)}, u32[]{:S(2)}) %all-to-all-start.1) | async-done | bytes 3407904 | tf_op jit(solution)/shard_map/all_to_all | solution.py:341
  158.3 0.0 copy-done.7
  158.3 0.0 copy-done.12
  158.3 0.0 copy-done.13
  158.3 1.9 %copy-done.3 = bf16[160,80,128]{2,1,0:T(8,128)(2,1)S(1)} copy-done((bf16[160,80,128]{2,1,0:T(8,128)(2,1)S(1)}, bf16[160,80,128]{2,1,0:T(8,128)(2,1)}, u32[]{:S(2)}) %copy-start.3) | copy-done | bytes 3276824
  160.2 5.5 %finish.1 = bf16[160,80,128]{2,1,0:T(8,128)(2,1)} custom-call(bf16[128,104,128]{2,1,0:T(8,128)(2,1)S(1)} %all-to-all-done.1.held, bf16[160,80,128]{2,1,0:T(8,128)(2,1)S(1)} %copy-done.3, f32[1,128]{1,0:T(1,128)S(1)} %bitcast.8, f32[1,128]{1,0:T(1,128)S(1)} %bitcast.9, bf16[128,128]{1,0:T(8,128)(2,1)S(1)} %copy-done.7), custom_call_target="tpu_custom_call" | custom-call | flops 419430400 | bytes 10485760 | tf_op jit(solution)/shard_map/finish/pallas_call | solution.py:315
  (11 shorter events, 0.0 us)
Async XLA Ops:
  0.0 1.9 %copy-start = (bf16[160,80,128]{2,1,0:T(8,128)(2,1)S(1)}, bf16[160,80,128]{2,1,0:T(8,128)(2,1)}, u32[]{:S(2)}) copy-start(bf16[160,80,128]{2,1,0:T(8,128)(2,1)} %pair_ref.3) | copy-start | bytes 9830404
  1.9 0.9 copy-start.5
  2.8 0.7 copy-start.8
  3.5 0.7 copy-start.10
  108.5 1.7 %copy-start.4 = (bf16[128,104,128]{2,1,0:T(8,128)(2,1)}, bf16[128,104,128]{2,1,0:T(8,128)(2,1)S(1)}, u32[]{:S(2)}) copy-start(bf16[128,104,128]{2,1,0:T(8,128)(2,1)S(1)} %triangle.1) | copy-start | bytes 10223620
  110.2 5.0 %copy-start.6 = (bf16[128,128]{1,0:T(8,128)(2,1)S(1)}, bf16[128,128]{1,0:T(8,128)(2,1)}, u32[]{:S(2)}) copy-start(bf16[128,128]{1,0:T(8,128)(2,1)} %weight_hbm.4) | copy-start | bytes 98308
  110.2 5.1 %copy-start.9 = (f32[128]{0:T(128)S(1)}, f32[128]{0:T(128)}, u32[]{:S(2)}) copy-start(f32[128]{0:T(128)} %param.9) | copy-start | bytes 1540
  110.2 5.1 %copy-start.11 = (f32[128]{0:T(128)S(1)}, f32[128]{0:T(128)}, u32[]{:S(2)}) copy-start(f32[128]{0:T(128)} %param.10) | copy-start | bytes 1540
  110.2 48.0 %all-to-all-start.1 = ((bf16[128,104,128]{2,1,0:T(8,128)(2,1)}), bf16[128,104,128]{2,1,0:T(8,128)(2,1)S(1)}, u32[]{:S(2)}, u32[]{:S(2)}) async-start(bf16[128,104,128]{2,1,0:T(8,128)(2,1)} %copy-done.4), calls=%async_computation.1 | async-start | bytes 6815744 | tf_op jit(solution)/shard_map/all_to_all | solution.py:341
  115.3 1.9 %copy-start.1 = (bf16[160,80,128]{2,1,0:T(8,128)(2,1)S(1)}, bf16[160,80,128]{2,1,0:T(8,128)(2,1)}, u32[]{:S(2)}) copy-start(bf16[160,80,128]{2,1,0:T(8,128)(2,1)} %pair_ref.3) | copy-start | bytes 9830404
  117.2 41.1 %copy-start.7 = (bf16[128,128]{1,0:T(8,128)(2,1)S(1)}, bf16[128,128]{1,0:T(8,128)(2,1)}, u32[]{:S(2)}) copy-start(bf16[128,128]{1,0:T(8,128)(2,1)} %weight_hbm.5) | copy-start | bytes 98308
  117.2 41.1 %copy-start.12 = (f32[128]{0:T(128)S(1)}, f32[128]{0:T(128)}, u32[]{:S(2)}) copy-start(f32[128]{0:T(128)} %param.13) | copy-start | bytes 1540
  117.2 41.1 %copy-start.13 = (f32[128]{0:T(128)S(1)}, f32[128]{0:T(128)}, u32[]{:S(2)}) copy-start(f32[128]{0:T(128)} %param.14) | copy-start | bytes 1540
  125.4 1.7 %copy-start.2 = (bf16[160,80,128]{2,1,0:T(8,128)(2,1)}, bf16[160,80,128]{2,1,0:T(8,128)(2,1)S(1)}, u32[]{:S(2)}) copy-start(bf16[160,80,128]{2,1,0:T(8,128)(2,1)S(1)} %gates.1.gate_ref) | copy-start | bytes 9830404
  158.3 1.9 %copy-start.3 = (bf16[160,80,128]{2,1,0:T(8,128)(2,1)S(1)}, bf16[160,80,128]{2,1,0:T(8,128)(2,1)}, u32[]{:S(2)}) copy-start(bf16[160,80,128]{2,1,0:T(8,128)(2,1)} %copy-done.2) | copy-start | bytes 9830404

commit v4 on v3

--- a/solution.py
+++ b/solution.py
@@ -53,6 +53,10 @@
     return centred * lax.rsqrt(var + 1e-05) * gain + bias
 
 
+def in_hbm(*arrays):
+    return [pltpu.with_memory_space_constraint(array, pltpu.HBM) for array in arrays]
+
+
 def fetch(sources, targets, sems):
     copies = [pltpu.make_async_copy(src, dst, sems.at[n]) for n, (src, dst) in enumerate(zip(sources, targets))]
     for copy in copies:
@@ -64,13 +68,10 @@
     pair_ref, gain_hbm, bias_hbm, weight_hbm, out_ref, gain_ref, bias_ref, weight_ref, weight_t, held, normed, dense,
     tail, sems, small_sems
 ):
-    loads = [
-        pltpu.make_async_copy(pair_ref.at[:, pl.ds(t * CHUNK, CHUNK), :], held.at[t], sems.at[t]) for t in range(CHUNKS)
-    ]
-    for load in loads:
-        load.start()
-    small = (gain_ref, bias_ref, weight_ref)
-    for copy in fetch((gain_hbm, bias_hbm, weight_hbm), small, small_sems):
+    small = fetch((gain_hbm, bias_hbm, weight_hbm), (gain_ref, bias_ref, weight_ref), small_sems)
+    for t in range(CHUNKS):
+        pltpu.make_async_copy(pair_ref.at[:, pl.ds(t * CHUNK, CHUNK), :], held.at[t], sems.at[t]).start()
+    for copy in small:
         copy.wait()
     for m in range(4):
         turned = (0.5 * weight_ref[:, m * C : (m + 1) * C].astype(F32)).T.astype(BF16)
@@ -144,11 +145,11 @@
         compiler_params=pltpu.CompilerParams(vmem_limit_bytes=VMEM_BYTES),
         cost_estimate=pl.CostEstimate(flops=2 * ROWS * COLS * C * 4 * C, bytes_accessed=10 * MIB, transcendentals=0),
         name="edges",
-    )(pair, gain[None, :], bias[None, :], weight)
+    )(*in_hbm(pair, gain[None, :], bias[None, :], weight))
 
 
 def gate_kernel(
-    pair_ref, gain_hbm, bias_hbm, weight_hbm, out_ref, gain_ref, bias_ref, weight_ref, held, sems
+    pair_ref, gain_hbm, bias_hbm, weight_hbm, out_hbm, gain_ref, bias_ref, weight_ref, held, out_ref, sems
 ):
     for copy in fetch((pair_ref, gain_hbm, bias_hbm, weight_hbm), (held, gain_ref, bias_ref, weight_ref), sems):
         copy.wait()
@@ -162,25 +163,30 @@
         value = jax.nn.sigmoid(jnp.dot(normed, weight, preferred_element_type=F32))
         out_ref[pl.ds(n * group, group)] = value.astype(BF16).reshape(group, COLS, C)
 
+    store = pltpu.make_async_copy(out_ref, out_hbm, sems.at[4])
+    store.start()
+    store.wait()
+
 
 def gates(pair, gain, bias, weight):
-    vmem, hbm = pl.BlockSpec(memory_space=pltpu.VMEM), pl.BlockSpec(memory_space=pltpu.HBM)
+    hbm = pl.BlockSpec(memory_space=pltpu.HBM)
     return pl.pallas_call(
         gate_kernel,
         in_specs=[hbm] * 4,
-        out_specs=vmem,
-        out_shape=jax.ShapeDtypeStruct((ROWS, COLS, C), BF16),
+        out_specs=hbm,
+        out_shape=pltpu.HBM((ROWS, COLS, C), BF16),
         scratch_shapes=[
             pltpu.VMEM((1, C), F32),
             pltpu.VMEM((1, C), F32),
             pltpu.VMEM((C, C), BF16),
             pltpu.VMEM((ROWS, COLS, C), BF16),
-            pltpu.SemaphoreType.DMA((4,)),
+            pltpu.VMEM((ROWS, COLS, C), BF16),
+            pltpu.SemaphoreType.DMA((5,)),
         ],
         compiler_params=pltpu.CompilerParams(vmem_limit_bytes=VMEM_BYTES),
         cost_estimate=pl.CostEstimate(flops=2 * ROWS * COLS * C * C, bytes_accessed=30 * MIB, transcendentals=0),
         name="gates",
-    )(pair, gain[None, :], bias[None, :], weight)
+    )(*in_hbm(pair, gain[None, :], bias[None, :], weight))
 
 
 def regroup(pieces, lane):
@@ -195,7 +201,7 @@
     return out
 
 
-def triangle_kernel(edges_ref, out_ref, left_rest, right_t, rest_left, rest_right, tri_rest):
+def triangle_kernel(edges_ref, out_hbm, left_rest, right_t, rest_left, rest_right, tri_rest, out_ref, sem):
     lane = lax.broadcasted_iota(jnp.int32, (2 * TAIL, LANES), 1)
     for c in range(N_CHAN):
         for q in range(N_ROW // PACK):
@@ -223,8 +229,9 @@
         tri_rest[q] = part[:, q * LANES : (q + 1) * LANES]
     lane = lax.broadcasted_iota(jnp.int32, (TAIL, LANES), 1)
     for n in range(N_ROW // 2):
-        for c in range(4 * n, 4 * n + 4):
-            for q in range(N_ROW // PACK):
+        q = n // 2
+        if n % 2 == 0:
+            for c in range(N_CHAN):
                 pieces = [tri_rest[q, pl.ds(c * COLS + b, TAIL, stride=PACK), :] for b in range(PACK)]
                 for a, value in enumerate(regroup(pieces, lane)):
                     value = jnp.concatenate([value, jnp.zeros((BACK - COLS - TAIL, LANES), F32)], axis=0)
@@ -234,9 +241,10 @@
         for e in range(2):
             r = 2 * n + e
             for c in range(N_CHAN):
-                out_ref[BACK_TO_BLOCK[r * N_CHAN + c], :COLS, :] = part[
-                    c * COLS : (c + 1) * COLS, e * LANES : (e + 1) * LANES
-                ]
+                to = BACK_TO_BLOCK[r * N_CHAN + c]
+                out_ref[to, :COLS, :] = part[c * COLS : (c + 1) * COLS, e * LANES : (e + 1) * LANES]
+                pltpu.make_async_copy(out_ref.at[to], out_hbm.at[to], sem).start()
+    pltpu.make_async_copy(out_ref, out_hbm, sem).wait()
 
 
 def triangle(edges_all):
@@ -244,14 +252,16 @@
     return pl.pallas_call(
         triangle_kernel,
         in_specs=[vmem],
-        out_specs=vmem,
-        out_shape=jax.ShapeDtypeStruct((N_ROW * N_CHAN, BACK, LANES), BF16),
+        out_specs=pl.BlockSpec(memory_space=pltpu.HBM),
+        out_shape=pltpu.HBM((N_ROW * N_CHAN, BACK, LANES), BF16),
         scratch_shapes=[
             pltpu.VMEM((SIDE, 2 * LANES), BF16),
             pltpu.VMEM((SIDE, SIDE), BF16),
             pltpu.VMEM((N_ROW // PACK, SIDE, LANES), F32),
             pltpu.VMEM((N_ROW // PACK, SIDE, LANES), F32),
             pltpu.VMEM((N_ROW // PACK, SIDE, LANES), F32),
+            pltpu.VMEM((N_ROW * N_CHAN, BACK, LANES), BF16),
+            pltpu.SemaphoreType.DMA,
         ],
         compiler_params=pltpu.CompilerParams(vmem_limit_bytes=VMEM_BYTES),
         cost_estimate=pl.CostEstimate(flops=2 * SIDE**3, bytes_accessed=10 * MIB, transcendentals=0),
@@ -260,18 +270,30 @@
 
 
 def finish_kernel(
-    held, gate_ref, gain_hbm, bias_hbm, weight_hbm, out_ref, gain_ref, bias_ref, weight_ref, wide, dense, tail, done,
+    held, gate_hbm, gain_hbm, bias_hbm, weight_hbm, out_ref, gate_ref, gain_ref, bias_ref, weight_ref, wide, dense, tail, done,
     sems, small_sems
 ):
     def store(t):
         rows = pl.ds(pl.multiple_of(t * CHUNK, CHUNK), CHUNK)
         return pltpu.make_async_copy(
-            done.at[pl.ds(0, LANES), rows, :], out_ref.at[pl.ds(0, LANES), rows, :], sems.at[0]
+            done.at[pl.ds(0, LANES), rows, :], out_ref.at[pl.ds(0, LANES), rows, :], sems.at[CHUNKS + 1]
         )
 
+    def load(t):
+        rows = pl.ds(pl.multiple_of(t * CHUNK, CHUNK), CHUNK)
+        return pltpu.make_async_copy(
+            gate_hbm.at[pl.ds(0, LANES), rows, :], gate_ref.at[pl.ds(0, LANES), rows, :], sems.at[t]
+        )
+
     rest = pl.ds(LANES, REST)
-    small = (gain_ref, bias_ref, weight_ref)
-    for copy in fetch((gain_hbm, bias_hbm, weight_hbm), small, small_sems):
+    small = fetch((gain_hbm, bias_hbm, weight_hbm), (gain_ref, bias_ref, weight_ref), small_sems)
+    for t in range(CHUNKS):
+        load(t).start()
+    gate_tail = pltpu.make_async_copy(gate_hbm.at[rest], gate_ref.at[rest], sems.at[CHUNKS])
+    gate_tail.start()
+    for h in range(C):
+        wide[h * STEP : h * STEP + TAIL, :] = held[h, COLS:, :].astype(F32)[:TAIL]
+    for copy in small:
         copy.wait()
     gain = jnp.broadcast_to(gain_ref[...], (LANES, C)).T
     bias = jnp.broadcast_to(bias_ref[...], (LANES, C)).T
@@ -281,8 +303,6 @@
         normed = layer_norm(wide[pl.ds(g, C, stride=STEP), :], gain, bias, 0).astype(BF16)
         return lax.dot_general(normed, weight, (((0,), (0,)), ((), ())), preferred_element_type=F32)
 
-    for h in range(C):
-        wide[h * STEP : h * STEP + TAIL, :] = held[h, COLS:, :].astype(F32)[:TAIL]
     for m in range(TAIL):
         value = project(m)
         for e in range(PACK):
@@ -290,6 +310,7 @@
 
     @pl.loop(0, CHUNKS)
     def _(t):
+        load(t).wait()
         to = pl.multiple_of(t * CHUNK, CHUNK)
         for h in range(C):
             wide[h * STEP : h * STEP + CHUNK, :] = held[h, pl.ds(to, CHUNK), :].astype(F32)
@@ -300,10 +321,11 @@
             done[i, pl.ds(to, CHUNK), :] = (gate * dense[i * STEP : i * STEP + CHUNK, :]).astype(BF16)
         store(t).start()
 
+    gate_tail.wait()
     for i in range(REST):
         gate = gate_ref[LANES + i].astype(F32)
         done[LANES + i] = (gate * tail[i * COLS_STEP : i * COLS_STEP + COLS, :]).astype(BF16)
-    last = pltpu.make_async_copy(done.at[rest], out_ref.at[rest], sems.at[1])
+    last = pltpu.make_async_copy(done.at[rest], out_ref.at[rest], sems.at[CHUNKS + 2])
     last.start()
     last.wait()
     for t in range(CHUNKS):
@@ -314,10 +336,11 @@
     vmem, hbm = pl.BlockSpec(memory_space=pltpu.VMEM), pl.BlockSpec(memory_space=pltpu.HBM)
     return pl.pallas_call(
         finish_kernel,
-        in_specs=[vmem, vmem, hbm, hbm, hbm],
+        in_specs=[vmem, hbm, hbm, hbm, hbm],
         out_specs=hbm,
         out_shape=jax.ShapeDtypeStruct((ROWS, COLS, C), BF16),
         scratch_shapes=[
+            pltpu.VMEM((ROWS, COLS, C), BF16),
             pltpu.VMEM((1, C), F32),
             pltpu.VMEM((1, C), F32),
             pltpu.VMEM((C, C), BF16),
@@ -325,13 +348,13 @@
             pltpu.VMEM((LANES * STEP, C), F32),
             pltpu.VMEM((REST * COLS_STEP, C), F32),
             pltpu.VMEM((ROWS, COLS, C), BF16),
-            pltpu.SemaphoreType.DMA((2,)),
+            pltpu.SemaphoreType.DMA((CHUNKS + 3,)),
             pltpu.SemaphoreType.DMA((3,)),
         ],
         compiler_params=pltpu.CompilerParams(vmem_limit_bytes=VMEM_BYTES),
         cost_estimate=pl.CostEstimate(flops=2 * ROWS * COLS * C * C, bytes_accessed=10 * MIB, transcendentals=0),
         name="finish",
-    )(tri, gate, gain[None, :], bias[None, :], weight)
+    )(tri, *in_hbm(gate, gain[None, :], bias[None, :], weight))
 
 
 def shards(pair, in_gain, in_bias, edge_weight, gate_weight, out_gain, out_bias, out_weight):

time: 166 us -> 162 us (0.976)
  local copies, waits for them, and re-layouts: 11.4 us -> 0 us
  Pallas kernels: 27.3 us -> 34.5 us
    unnamed x28 -> x0, local copies, waits for them, and re-layouts: 11.4 us -> none
    pallas_call x3, Pallas kernels: 19.5 us -> 25.3 us  [the longest x1 11.4 us: gates(): pl.pallas_call(gate_kernel, in_specs=[hbm] * 4, out_specs=hbm, out_shape=...]
  transfers between devices with their start and end apart: 1 -> 1, of which waited for: 1 -> 1; matrix products, arithmetic and copies ran while one was open for 0% -> 0% of each run, Pallas kernels for 5% -> 7%
where the time goes in v4:
time: 162 us
  blocking collectives  90.6 us (56%)
  Pallas kernels  34.5 us (21%)
  waiting for transfers between devices  31.6 us (20%)
  starting transfers between devices  5.03 us (3%)
    all_to_all x1, blocking collectives, shards(): lax.all_to_all(both, OUT_ORDER, split_axis=0, concat_axis=0, tiled=True)  90.6 us
    all_to_all x1, waiting for transfers between devices, shards(): lax.all_to_all(triangle(both_all), BACK_ORDER, split_axis=0, concat_axis=...  31.6 us
    pallas_call x1, Pallas kernels, gates(): pl.pallas_call(gate_kernel, in_specs=[hbm] * 4, out_specs=hbm, out_shape=...  11.4 us
    pallas_call x1, Pallas kernels, edges(): pl.pallas_call(edges_kernel, in_specs=[hbm] * 4, out_specs=vmem, out_shap...  9.2 us
    pallas_call x1, Pallas kernels, triangle(): pl.pallas_call(triangle_kernel, in_specs=[vmem], out_specs=pl.BlockSpec(m...  7.02 us
    pallas_call x1, Pallas kernels, finish(): pl.pallas_call(finish_kernel, in_specs=[vmem, hbm, hbm, hbm, hbm], out_sp...  6.93 us
    all_to_all x1, starting transfers between devices, shards(): lax.all_to_all(triangle(both_all), BACK_ORDER, split_axis=0, concat_axis=...  5.03 us
  transfers between devices with their start and end apart: 1, of which 1 were waited for; matrix products, arithmetic and copies ran while one was open for 0% of the time, Pallas kernels for 7%

profile of v4, /device:TPU:1, one launch (start us, length us, event | category | flops | bytes accessed | tf_op | source)
XLA Modules:
  0.0 161.9 jit_solution(18332254333464283762)
XLA Ops:
  0.0 9.2 %edges.1 = bf16[128,200,128]{2,1,0:T(8,128)(2,1)S(1)} custom-call(bf16[160,80,128]{2,1,0:T(8,128)(2,1)} %pair_ref.3, f32[1,128]{1,0:T(1,128)} %bitcast.4, f32[1,128]{1,0:T(1,128)} %bitcast.6, bf16[128,512]{1,0:T(8,128)(2,1)} %weight_hbm.3), custom_call_target="tpu_custom_call" | custom-call | flops 1677721600 | bytes 10485760 | tf_op jit(solution)/shard_map/edges/pallas_call | solution.py:128
  9.2 90.6 %all_to_all.10.edges_ref = bf16[128,200,128]{2,1,0:T(8,128)(2,1)S(1)} all-to-all(bf16[128,200,128]{2,1,0:T(8,128)(2,1)S(1)} %edges.1), channel_id=1, replica_groups=mesh['y'=4,'z_lo'=2,'core'=2,'z_hi'=2,'x'=4] {'z_hi','x','y','z_lo','core'}, dimensions={0} | all-to-all | bytes 13107200 | tf_op jit(solution)/shard_map/all_to_all | solution.py:362
  99.9 7.0 %triangle.1 = bf16[128,104,128]{2,1,0:T(8,128)(2,1)} custom-call(bf16[128,200,128]{2,1,0:T(8,128)(2,1)S(1)} %all_to_all.10.edges_ref), custom_call_target="tpu_custom_call" | custom-call | flops 4194304000 | bytes 10485760 | tf_op jit(solution)/shard_map/triangle/pallas_call | solution.py:252
  106.9 5.0 %all-to-all-start.1 = ((bf16[128,104,128]{2,1,0:T(8,128)(2,1)}), bf16[128,104,128]{2,1,0:T(8,128)(2,1)S(1)}, u32[]{:S(2)}, u32[]{:S(2)}) async-start(bf16[128,104,128]{2,1,0:T(8,128)(2,1)} %triangle.1), calls=%async_computation.1 | async-start | bytes 6815744 | tf_op jit(solution)/shard_map/all_to_all | solution.py:364
  111.9 11.4 %gates.1.gate_hbm = bf16[160,80,128]{2,1,0:T(8,128)(2,1)} custom-call(bf16[160,80,128]{2,1,0:T(8,128)(2,1)} %pair_ref.3, f32[1,128]{1,0:T(1,128)} %bitcast.5, f32[1,128]{1,0:T(1,128)} %bitcast.7, bf16[128,128]{1,0:T(8,128)(2,1)} %weight_hbm.4), custom_call_target="tpu_custom_call" | custom-call | flops 419430400 | bytes 31457280 | tf_op jit(solution)/shard_map/gates/pallas_call | solution.py:173
  123.3 31.6 %all-to-all-done.1.held = bf16[128,104,128]{2,1,0:T(8,128)(2,1)S(1)} async-done(((bf16[128,104,128]{2,1,0:T(8,128)(2,1)}), bf16[128,104,128]{2,1,0:T(8,128)(2,1)S(1)}, u32[]{:S(2)}, u32[]{:S(2)}) %all-to-all-start.1) | async-done | bytes 3407904 | tf_op jit(solution)/shard_map/all_to_all | solution.py:364
  154.9 6.9 %finish.1 = bf16[160,80,128]{2,1,0:T(8,128)(2,1)} custom-call(bf16[128,104,128]{2,1,0:T(8,128)(2,1)S(1)} %all-to-all-done.1.held, bf16[160,80,128]{2,1,0:T(8,128)(2,1)} %gates.1.gate_hbm, f32[1,128]{1,0:T(1,128)} %bitcast.8, f32[1,128]{1,0:T(1,128)} %bitcast.9, bf16[128,128]{1,0:T(8,128)(2,1)} %weight_hbm.5), custom_call_target="tpu_custom_call" | custom-call | flops 419430400 | bytes 10485760 | tf_op jit(solution)/shard_map/finish/pallas_call | solution.py:337
Async XLA Ops:
  106.9 48.0 %all-to-all-start.1 = ((bf16[128,104,128]{2,1,0:T(8,128)(2,1)}), bf16[128,104,128]{2,1,0:T(8,128)(2,1)S(1)}, u32[]{:S(2)}, u32[]{:S(2)}) async-start(bf16[128,104,128]{2,1,0:T(8,128)(2,1)} %triangle.1), calls=%async_computation.1 | async-start | bytes 6815744 | tf_op jit(solution)/shard_map/all_to_all | solution.py:364

commit v5 on v4

--- a/solution.py
+++ b/solution.py
@@ -18,6 +18,7 @@
 BOTH = 2 * (COLS + TAIL)
 BACK = 104
 N_ROW, N_CHAN = 8, 16
+HALF = N_CHAN // 2
 SIZES = {"y": 4, "z_lo": 2, "core": 2, "z_hi": 2, "x": 4}
 ROW, CHAN = ("z_hi", "x"), ("y", "z_lo", "core")
 OUT_ORDER = ROW + CHAN
@@ -74,11 +75,13 @@
     for copy in small:
         copy.wait()
     for m in range(4):
-        turned = (0.5 * weight_ref[:, m * C : (m + 1) * C].astype(F32)).T.astype(BF16)
+        columns = (0.5 * weight_ref[:, m * C : (m + 1) * C].astype(F32)).T.astype(BF16)
         for b in range(C // 16):
             at = 2 * C * (m // 2) + 32 * b + 16 * (m % 2)
-            weight_t[at : at + 16, :] = turned[16 * b : 16 * b + 16]
+            weight_t[at : at + 16, :] = columns[16 * b : 16 * b + 16]
     gain, bias = gain_ref[...], bias_ref[...]
+    average = jnp.full((C, C), 1 / C, BF16)
+    turn = lax.axis_index("x")
 
     def product(x, side):
         both = lax.dot_general(
@@ -92,8 +95,10 @@
         pltpu.make_async_copy(pair_ref.at[:, pl.ds(t * CHUNK, CHUNK), :], held.at[t], sems.at[t]).wait()
         group = 8
         for n in range(ROWS // group):
-            block = held[t, n * group : (n + 1) * group].reshape(group * CHUNK, C).astype(F32)
-            block = layer_norm(block, gain, bias, -1)
+            block = held[t, n * group : (n + 1) * group].reshape(group * CHUNK, C)
+            centred = block.astype(F32) - jnp.dot(block, average, preferred_element_type=F32)
+            var = jnp.mean(centred * centred, axis=-1, keepdims=True)
+            block = centred * lax.rsqrt(var + 1e-05) * gain + bias
             for u in range(group):
                 at = (n * group + u) * STEP
                 normed[at : at + CHUNK, :] = block[u * CHUNK : (u + 1) * CHUNK]
@@ -107,7 +112,12 @@
                     dense[side, pl.ds(2 * n + e, C, stride=STEP), :] = value[:, e * 128 : (e + 1) * 128]
         for n in range(CHUNK // 8):
             x = jnp.concatenate(
-                [normed[pl.ds(LANES * STEP + 8 * n + e, REST, stride=STEP), :] for e in range(8)], axis=0
+                [
+                    normed[pl.ds(LANES * STEP + 8 * n + u + lax.rem(g + PACK - turn, PACK), REST, stride=STEP), :]
+                    for u in (0, PACK)
+                    for g in range(PACK)
+                ],
+                axis=0,
             ).astype(BF16)
             for side in range(2):
                 value = product(x, side)
@@ -189,16 +199,15 @@
     )(*in_hbm(pair, gain[None, :], bias[None, :], weight))
 
 
-def regroup(pieces, lane):
-    out = []
-    for b in range(PACK):
-        total = None
-        for a in range(PACK):
-            shift = ((a - b) * REST) % LANES
-            moved = pltpu.roll(pieces[a], shift, 1) if shift else pieces[a]
-            total = moved if total is None else jnp.where(lane // REST == a, moved, total)
-        out.append(total)
+def choose(lane, pieces):
+    out = pieces[0]
+    for g in range(1, PACK):
+        out = jnp.where(lane // REST == g, pieces[g], out)
     return out
+
+
+def turned(value, groups):
+    return pltpu.roll(value, groups * REST, 1) if groups else value
 
 
 def triangle_kernel(edges_ref, out_hbm, left_rest, right_t, rest_left, rest_right, tri_rest, out_ref, sem):
@@ -207,7 +216,8 @@
         for q in range(N_ROW // PACK):
             blocks = [FROM_BLOCK[(q * PACK + a) * N_CHAN + c] for a in range(PACK)]
             pieces = [edges_ref[block, 2 * COLS :, :].astype(F32) for block in blocks]
-            for b, value in enumerate(regroup(pieces, lane)):
+            for b in range(PACK):
+                value = turned(choose(lane, [pieces[(g - b) % PACK] for g in range(PACK)]), -b % PACK)
                 rest_left[q, pl.ds(c * COLS + b, TAIL, stride=PACK), :] = value[:TAIL]
                 rest_right[q, pl.ds(c * COLS + b, TAIL, stride=PACK), :] = value[TAIL:]
 
@@ -217,33 +227,38 @@
 
     for q in range(N_ROW // PACK):
         left_rest[:, q * LANES : (q + 1) * LANES] = rest_left[q].astype(BF16)
-        turned = rest_right[q].astype(BF16).T
+        columns = rest_right[q].astype(BF16).T
         for a in range(PACK):
             at = (q * PACK + a) * ROWS + LANES
-            right_t[at : at + REST, :] = turned[a * REST : (a + 1) * REST]
+            right_t[at : at + REST, :] = columns[a * REST : (a + 1) * REST]
     for r in range(N_ROW):
         right_t[r * ROWS : r * ROWS + LANES, :] = side(r, COLS).T
 
-    part = jnp.dot(right_t[...], left_rest[...], preferred_element_type=F32)
-    for q in range(N_ROW // PACK):
-        tri_rest[q] = part[:, q * LANES : (q + 1) * LANES]
+    for first in range(0, N_CHAN, HALF):
+        rows = pl.ds(first * COLS, HALF * COLS)
+        part = jnp.dot(right_t[rows, :], left_rest[...], preferred_element_type=F32)
+        for q in range(N_ROW // PACK):
+            tri_rest[q, rows, :] = part[:, q * LANES : (q + 1) * LANES]
     lane = lax.broadcasted_iota(jnp.int32, (TAIL, LANES), 1)
     for n in range(N_ROW // 2):
         q = n // 2
         if n % 2 == 0:
             for c in range(N_CHAN):
                 pieces = [tri_rest[q, pl.ds(c * COLS + b, TAIL, stride=PACK), :] for b in range(PACK)]
-                for a, value in enumerate(regroup(pieces, lane)):
+                pieces = [turned(piece, b) for b, piece in enumerate(pieces)]
+                for a in range(PACK):
+                    value = choose(lane, [pieces[(g - a) % PACK] for g in range(PACK)])
                     value = jnp.concatenate([value, jnp.zeros((BACK - COLS - TAIL, LANES), F32)], axis=0)
                     out_ref[BACK_TO_BLOCK[(q * PACK + a) * N_CHAN + c], COLS:, :] = value.astype(BF16)
         pair = jnp.concatenate([side(2 * n, 0), side(2 * n + 1, 0)], axis=1)
-        part = jnp.dot(right_t[...], pair, preferred_element_type=F32).astype(BF16)
-        for e in range(2):
-            r = 2 * n + e
-            for c in range(N_CHAN):
-                to = BACK_TO_BLOCK[r * N_CHAN + c]
-                out_ref[to, :COLS, :] = part[c * COLS : (c + 1) * COLS, e * LANES : (e + 1) * LANES]
-                pltpu.make_async_copy(out_ref.at[to], out_hbm.at[to], sem).start()
+        for first in range(0, N_CHAN, HALF):
+            rows = right_t[first * COLS : (first + HALF) * COLS]
+            part = jnp.dot(rows, pair, preferred_element_type=F32).astype(BF16)
+            for e in range(2):
+                for c in range(HALF):
+                    to = BACK_TO_BLOCK[(2 * n + e) * N_CHAN + first + c]
+                    out_ref[to, :COLS, :] = part[c * COLS : (c + 1) * COLS, e * LANES : (e + 1) * LANES]
+                    pltpu.make_async_copy(out_ref.at[to], out_hbm.at[to], sem).start()
     pltpu.make_async_copy(out_ref, out_hbm, sem).wait()
 
 
@@ -287,10 +302,11 @@
 
     rest = pl.ds(LANES, REST)
     small = fetch((gain_hbm, bias_hbm, weight_hbm), (gain_ref, bias_ref, weight_ref), small_sems)
+    gate_tail = pltpu.make_async_copy(gate_hbm.at[rest], gate_ref.at[rest], sems.at[CHUNKS])
+    gate_tail.start()
     for t in range(CHUNKS):
         load(t).start()
-    gate_tail = pltpu.make_async_copy(gate_hbm.at[rest], gate_ref.at[rest], sems.at[CHUNKS])
-    gate_tail.start()
+    turn = lax.axis_index("x")
     for h in range(C):
         wide[h * STEP : h * STEP + TAIL, :] = held[h, COLS:, :].astype(F32)[:TAIL]
     for copy in small:
@@ -305,8 +321,15 @@
 
     for m in range(TAIL):
         value = project(m)
-        for e in range(PACK):
-            tail[pl.ds(PACK * m + e, REST, stride=COLS_STEP), :] = value[e * REST : (e + 1) * REST]
+        for g in range(PACK):
+            at = PACK * m + lax.rem(g + PACK - turn, PACK)
+            tail[pl.ds(at, REST, stride=COLS_STEP), :] = value[g * REST : (g + 1) * REST]
+    gate_tail.wait()
+    for i in range(REST):
+        gate = gate_ref[LANES + i].astype(F32)
+        done[LANES + i] = (gate * tail[i * COLS_STEP : i * COLS_STEP + COLS, :]).astype(BF16)
+    last = pltpu.make_async_copy(done.at[rest], out_ref.at[rest], sems.at[CHUNKS + 2])
+    last.start()
 
     @pl.loop(0, CHUNKS)
     def _(t):
@@ -321,12 +344,6 @@
             done[i, pl.ds(to, CHUNK), :] = (gate * dense[i * STEP : i * STEP + CHUNK, :]).astype(BF16)
         store(t).start()
 
-    gate_tail.wait()
-    for i in range(REST):
-        gate = gate_ref[LANES + i].astype(F32)
-        done[LANES + i] = (gate * tail[i * COLS_STEP : i * COLS_STEP + COLS, :]).astype(BF16)
-    last = pltpu.make_async_copy(done.at[rest], out_ref.at[rest], sems.at[CHUNKS + 2])
-    last.start()
     last.wait()
     for t in range(CHUNKS):
         store(t).wait()

time: 162 us -> 161 us (level)
  no operation moved by 1% of the time
where the time goes in v5:
time: 161 us
  blocking collectives  90.7 us (56%)
  Pallas kernels  33.4 us (21%)
  waiting for transfers between devices  31.6 us (20%)
  starting transfers between devices  5.03 us (3%)
    all_to_all x1, blocking collectives, shards(): lax.all_to_all(both, OUT_ORDER, split_axis=0, concat_axis=0, tiled=True)  90.7 us
    all_to_all x1, waiting for transfers between devices, shards(): lax.all_to_all(triangle(both_all), BACK_ORDER, split_axis=0, concat_axis=...  31.6 us
    pallas_call x1, Pallas kernels, gates(): pl.pallas_call(gate_kernel, in_specs=[hbm] * 4, out_specs=hbm, out_shape=...  11.4 us
    pallas_call x1, Pallas kernels, edges(): pl.pallas_call(edges_kernel, in_specs=[hbm] * 4, out_specs=vmem, out_shap...  9.02 us
    pallas_call x1, Pallas kernels, finish(): pl.pallas_call(finish_kernel, in_specs=[vmem, hbm, hbm, hbm, hbm], out_sp...  6.82 us
    pallas_call x1, Pallas kernels, triangle(): pl.pallas_call(triangle_kernel, in_specs=[vmem], out_specs=pl.BlockSpec(m...  6.18 us
    all_to_all x1, starting transfers between devices, shards(): lax.all_to_all(triangle(both_all), BACK_ORDER, split_axis=0, concat_axis=...  5.03 us
  transfers between devices with their start and end apart: 1, of which 1 were waited for; matrix products, arithmetic and copies ran while one was open for 0% of the time, Pallas kernels for 7%

profile of v5, /device:TPU:1, one launch (start us, length us, event | category | flops | bytes accessed | tf_op | source)
XLA Modules:
  0.0 160.7 jit_solution(9213601864258465822)
XLA Ops:
  0.0 9.0 %edges.1 = bf16[128,200,128]{2,1,0:T(8,128)(2,1)S(1)} custom-call(bf16[160,80,128]{2,1,0:T(8,128)(2,1)} %pair_ref.3, f32[1,128]{1,0:T(1,128)} %bitcast.4, f32[1,128]{1,0:T(1,128)} %bitcast.6, bf16[128,512]{1,0:T(8,128)(2,1)} %weight_hbm.3), custom_call_target="tpu_custom_call" | custom-call | flops 1677721600 | bytes 10485760 | tf_op jit(solution)/shard_map/edges/pallas_call | solution.py:138
  9.0 90.7 %all_to_all.10.edges_ref = bf16[128,200,128]{2,1,0:T(8,128)(2,1)S(1)} all-to-all(bf16[128,200,128]{2,1,0:T(8,128)(2,1)S(1)} %edges.1), channel_id=1, replica_groups=mesh['y'=4,'z_lo'=2,'core'=2,'z_hi'=2,'x'=4] {'z_hi','x','y','z_lo','core'}, dimensions={0} | all-to-all | bytes 13107200 | tf_op jit(solution)/shard_map/all_to_all | solution.py:379
  99.7 6.2 %triangle.1 = bf16[128,104,128]{2,1,0:T(8,128)(2,1)} custom-call(bf16[128,200,128]{2,1,0:T(8,128)(2,1)S(1)} %all_to_all.10.edges_ref), custom_call_target="tpu_custom_call" | custom-call | flops 4194304000 | bytes 10485760 | tf_op jit(solution)/shard_map/triangle/pallas_call | solution.py:267
  105.9 5.0 %all-to-all-start.1 = ((bf16[128,104,128]{2,1,0:T(8,128)(2,1)}), bf16[128,104,128]{2,1,0:T(8,128)(2,1)S(1)}, u32[]{:S(2)}, u32[]{:S(2)}) async-start(bf16[128,104,128]{2,1,0:T(8,128)(2,1)} %triangle.1), calls=%async_computation.1 | async-start | bytes 6815744 | tf_op jit(solution)/shard_map/all_to_all | solution.py:381
  110.9 11.4 %gates.1.gate_hbm = bf16[160,80,128]{2,1,0:T(8,128)(2,1)} custom-call(bf16[160,80,128]{2,1,0:T(8,128)(2,1)} %pair_ref.3, f32[1,128]{1,0:T(1,128)} %bitcast.5, f32[1,128]{1,0:T(1,128)} %bitcast.7, bf16[128,128]{1,0:T(8,128)(2,1)} %weight_hbm.4), custom_call_target="tpu_custom_call" | custom-call | flops 419430400 | bytes 31457280 | tf_op jit(solution)/shard_map/gates/pallas_call | solution.py:183
  122.3 31.6 %all-to-all-done.1.held = bf16[128,104,128]{2,1,0:T(8,128)(2,1)S(1)} async-done(((bf16[128,104,128]{2,1,0:T(8,128)(2,1)}), bf16[128,104,128]{2,1,0:T(8,128)(2,1)S(1)}, u32[]{:S(2)}, u32[]{:S(2)}) %all-to-all-start.1) | async-done | bytes 3407904 | tf_op jit(solution)/shard_map/all_to_all | solution.py:381
  153.9 6.8 %finish.1 = bf16[160,80,128]{2,1,0:T(8,128)(2,1)} custom-call(bf16[128,104,128]{2,1,0:T(8,128)(2,1)S(1)} %all-to-all-done.1.held, bf16[160,80,128]{2,1,0:T(8,128)(2,1)} %gates.1.gate_hbm, f32[1,128]{1,0:T(1,128)} %bitcast.8, f32[1,128]{1,0:T(1,128)} %bitcast.9, bf16[128,128]{1,0:T(8,128)(2,1)} %weight_hbm.5), custom_call_target="tpu_custom_call" | custom-call | flops 419430400 | bytes 10485760 | tf_op jit(solution)/shard_map/finish/pallas_call | solution.py:354
Async XLA Ops:
  105.9 48.0 %all-to-all-start.1 = ((bf16[128,104,128]{2,1,0:T(8,128)(2,1)}), bf16[128,104,128]{2,1,0:T(8,128)(2,1)S(1)}, u32[]{:S(2)}, u32[]{:S(2)}) async-start(bf16[128,104,128]{2,1,0:T(8,128)(2,1)} %triangle.1), calls=%async_computation.1 | async-start | bytes 6815744 | tf_op jit(solution)/shard_map/all_to_all | solution.py:381

commit v6 on v5

--- a/solution.py
+++ b/solution.py
@@ -21,7 +21,7 @@
 HALF = N_CHAN // 2
 SIZES = {"y": 4, "z_lo": 2, "core": 2, "z_hi": 2, "x": 4}
 ROW, CHAN = ("z_hi", "x"), ("y", "z_lo", "core")
-OUT_ORDER = ROW + CHAN
+OUT_ORDER = ("z_hi", "x", "core", "y", "z_lo")
 BACK_ORDER = ("y", "x", "core", "z_lo", "z_hi")
 SIDE = 1280
 F32, BF16 = jnp.float32, jnp.bfloat16
@@ -93,7 +93,7 @@
     @pl.loop(0, CHUNKS)
     def _(t):
         pltpu.make_async_copy(pair_ref.at[:, pl.ds(t * CHUNK, CHUNK), :], held.at[t], sems.at[t]).wait()
-        group = 8
+        group = 16
         for n in range(ROWS // group):
             block = held[t, n * group : (n + 1) * group].reshape(group * CHUNK, C)
             centred = block.astype(F32) - jnp.dot(block, average, preferred_element_type=F32)
@@ -124,9 +124,9 @@
                 for e in range(2):
                     at = side * TAIL + 4 * t + 2 * n + e
                     tail[pl.ds(at, C, stride=TAIL_STEP), :] = value[:, e * 128 : (e + 1) * 128]
-        for side in range(2):
-            to = pl.multiple_of(side * COLS + t * CHUNK, CHUNK)
-            for h in range(C):
+        for h in range(C):
+            for side in range(2):
+                to = pl.multiple_of(side * COLS + t * CHUNK, CHUNK)
                 out_ref[OUT_OF_CHANNEL[h], pl.ds(to, CHUNK), :] = dense[side, h * STEP : h * STEP + CHUNK, :].astype(BF16)
 
     for h in range(C):

time: 161 us -> 160 us (level)
  blocking collectives: 90.7 us -> 88.1 us
  starting transfers between devices: 5.03 us -> 7.12 us
    all_to_all x1, blocking collectives: 90.7 us -> 88.1 us  [shards(): lax.all_to_all(both, OUT_ORDER, split_axis=0, concat_axis=0, tiled=True)]
    all_to_all x1, starting transfers between devices: 5.03 us -> 7.12 us  [shards(): lax.all_to_all(triangle(both_all), BACK_ORDER, split_axis=0, concat_axis=...]
where the time goes in v6:
time: 160 us
  blocking collectives  88.1 us (55%)
  Pallas kernels  33.1 us (21%)
  waiting for transfers between devices  31.6 us (20%)
  starting transfers between devices  7.12 us (4%)
    all_to_all x1, blocking collectives, shards(): lax.all_to_all(both, OUT_ORDER, split_axis=0, concat_axis=0, tiled=True)  88.1 us
    all_to_all x1, waiting for transfers between devices, shards(): lax.all_to_all(triangle(both_all), BACK_ORDER, split_axis=0, concat_axis=...  31.6 us
    pallas_call x1, Pallas kernels, gates(): pl.pallas_call(gate_kernel, in_specs=[hbm] * 4, out_specs=hbm, out_shape=...  11.4 us
    pallas_call x1, Pallas kernels, edges(): pl.pallas_call(edges_kernel, in_specs=[hbm] * 4, out_specs=vmem, out_shap...  8.68 us
    all_to_all x1, starting transfers between devices, shards(): lax.all_to_all(triangle(both_all), BACK_ORDER, split_axis=0, concat_axis=...  7.12 us
    pallas_call x1, Pallas kernels, finish(): pl.pallas_call(finish_kernel, in_specs=[vmem, hbm, hbm, hbm, hbm], out_sp...  6.82 us
    pallas_call x1, Pallas kernels, triangle(): pl.pallas_call(triangle_kernel, in_specs=[vmem], out_specs=pl.BlockSpec(m...  6.18 us
  transfers between devices with their start and end apart: 1, of which 1 were waited for; matrix products, arithmetic and copies ran while one was open for 0% of the time, Pallas kernels for 7%

profile of v6, /device:TPU:1, one launch (start us, length us, event | category | flops | bytes accessed | tf_op | source)
XLA Modules:
  0.0 160.0 jit_solution(13129181023784175988)
XLA Ops:
  0.0 8.7 %edges.1 = bf16[128,200,128]{2,1,0:T(8,128)(2,1)S(1)} custom-call(bf16[160,80,128]{2,1,0:T(8,128)(2,1)} %pair_ref.3, f32[1,128]{1,0:T(1,128)} %bitcast.4, f32[1,128]{1,0:T(1,128)} %bitcast.6, bf16[128,512]{1,0:T(8,128)(2,1)} %weight_hbm.3), custom_call_target="tpu_custom_call" | custom-call | flops 1677721600 | bytes 10485760 | tf_op jit(solution)/shard_map/edges/pallas_call | solution.py:138
  8.7 88.1 %all_to_all.10.edges_ref = bf16[128,200,128]{2,1,0:T(8,128)(2,1)S(1)} all-to-all(bf16[128,200,128]{2,1,0:T(8,128)(2,1)S(1)} %edges.1), channel_id=1, replica_groups=mesh['y'=4,'z_lo'=2,'core'=2,'z_hi'=2,'x'=4] {'z_hi','x','core','y','z_lo'}, dimensions={0} | all-to-all | bytes 13107200 | tf_op jit(solution)/shard_map/all_to_all | solution.py:379
  96.8 6.2 %triangle.1 = bf16[128,104,128]{2,1,0:T(8,128)(2,1)} custom-call(bf16[128,200,128]{2,1,0:T(8,128)(2,1)S(1)} %all_to_all.10.edges_ref), custom_call_target="tpu_custom_call" | custom-call | flops 4194304000 | bytes 10485760 | tf_op jit(solution)/shard_map/triangle/pallas_call | solution.py:267
  103.0 7.1 %all-to-all-start.1 = ((bf16[128,104,128]{2,1,0:T(8,128)(2,1)}), bf16[128,104,128]{2,1,0:T(8,128)(2,1)S(1)}, u32[]{:S(2)}, u32[]{:S(2)}) async-start(bf16[128,104,128]{2,1,0:T(8,128)(2,1)} %triangle.1), calls=%async_computation.1 | async-start | bytes 6815744 | tf_op jit(solution)/shard_map/all_to_all | solution.py:381
  110.1 11.4 %gates.1.gate_hbm = bf16[160,80,128]{2,1,0:T(8,128)(2,1)} custom-call(bf16[160,80,128]{2,1,0:T(8,128)(2,1)} %pair_ref.3, f32[1,128]{1,0:T(1,128)} %bitcast.5, f32[1,128]{1,0:T(1,128)} %bitcast.7, bf16[128,128]{1,0:T(8,128)(2,1)} %weight_hbm.4), custom_call_target="tpu_custom_call" | custom-call | flops 419430400 | bytes 31457280 | tf_op jit(solution)/shard_map/gates/pallas_call | solution.py:183
  121.5 31.6 %all-to-all-done.1.held = bf16[128,104,128]{2,1,0:T(8,128)(2,1)S(1)} async-done(((bf16[128,104,128]{2,1,0:T(8,128)(2,1)}), bf16[128,104,128]{2,1,0:T(8,128)(2,1)S(1)}, u32[]{:S(2)}, u32[]{:S(2)}) %all-to-all-start.1) | async-done | bytes 3407904 | tf_op jit(solution)/shard_map/all_to_all | solution.py:381
  153.1 6.8 %finish.1 = bf16[160,80,128]{2,1,0:T(8,128)(2,1)} custom-call(bf16[128,104,128]{2,1,0:T(8,128)(2,1)S(1)} %all-to-all-done.1.held, bf16[160,80,128]{2,1,0:T(8,128)(2,1)} %gates.1.gate_hbm, f32[1,128]{1,0:T(1,128)} %bitcast.8, f32[1,128]{1,0:T(1,128)} %bitcast.9, bf16[128,128]{1,0:T(8,128)(2,1)} %weight_hbm.5), custom_call_target="tpu_custom_call" | custom-call | flops 419430400 | bytes 10485760 | tf_op jit(solution)/shard_map/finish/pallas_call | solution.py:354
Async XLA Ops:
  103.0 50.1 %all-to-all-start.1 = ((bf16[128,104,128]{2,1,0:T(8,128)(2,1)}), bf16[128,104,128]{2,1,0:T(8,128)(2,1)S(1)}, u32[]{:S(2)}, u32[]{:S(2)}) async-start(bf16[128,104,128]{2,1,0:T(8,128)(2,1)} %triangle.1), calls=%async_computation.1 | async-start | bytes 6815744 | tf_op jit(solution)/shard_map/all_to_all | solution.py:381

commit v7 on v6

--- a/solution.py
+++ b/solution.py
@@ -15,6 +15,7 @@
 STEP = CHUNK + 4
 TAIL_STEP = 2 * TAIL + 4
 COLS_STEP = COLS + 4
+SPARE = 16
 BOTH = 2 * (COLS + TAIL)
 BACK = 104
 N_ROW, N_CHAN = 8, 16
@@ -226,8 +227,8 @@
         return jnp.concatenate([edges_ref[block, first : first + COLS, :] for block in blocks], axis=0)
 
     for q in range(N_ROW // PACK):
-        left_rest[:, q * LANES : (q + 1) * LANES] = rest_left[q].astype(BF16)
-        columns = rest_right[q].astype(BF16).T
+        left_rest[:, q * LANES : (q + 1) * LANES] = rest_left[q, :SIDE].astype(BF16)
+        columns = rest_right[q, :SIDE].astype(BF16).T
         for a in range(PACK):
             at = (q * PACK + a) * ROWS + LANES
             right_t[at : at + REST, :] = columns[a * REST : (a + 1) * REST]
@@ -272,9 +273,9 @@
         scratch_shapes=[
             pltpu.VMEM((SIDE, 2 * LANES), BF16),
             pltpu.VMEM((SIDE, SIDE), BF16),
-            pltpu.VMEM((N_ROW // PACK, SIDE, LANES), F32),
-            pltpu.VMEM((N_ROW // PACK, SIDE, LANES), F32),
-            pltpu.VMEM((N_ROW // PACK, SIDE, LANES), F32),
+            pltpu.VMEM((N_ROW // PACK, SIDE + SPARE, LANES), F32),
+            pltpu.VMEM((N_ROW // PACK, SIDE + SPARE, LANES), F32),
+            pltpu.VMEM((N_ROW // PACK, SIDE + SPARE, LANES), F32),
             pltpu.VMEM((N_ROW * N_CHAN, BACK, LANES), BF16),
             pltpu.SemaphoreType.DMA,
         ],
@@ -361,7 +362,7 @@
             pltpu.VMEM((1, C), F32),
             pltpu.VMEM((1, C), F32),
             pltpu.VMEM((C, C), BF16),
-            pltpu.VMEM((C * STEP, LANES), F32),
+            pltpu.VMEM((C * STEP + SPARE, LANES), F32),
             pltpu.VMEM((LANES * STEP, C), F32),
             pltpu.VMEM((REST * COLS_STEP, C), F32),
             pltpu.VMEM((ROWS, COLS, C), BF16),

time: 160 us -> 160 us (level)
  no operation moved by 1% of the time
where the time goes in v7:
time: 160 us
  blocking collectives  88.1 us (55%)
  Pallas kernels  33.1 us (21%)
  waiting for transfers between devices  31.6 us (20%)
  starting transfers between devices  7.12 us (4%)
    all_to_all x1, blocking collectives, shards(): lax.all_to_all(both, OUT_ORDER, split_axis=0, concat_axis=0, tiled=True)  88.1 us
    all_to_all x1, waiting for transfers between devices, shards(): lax.all_to_all(triangle(both_all), BACK_ORDER, split_axis=0, concat_axis=...  31.6 us
    pallas_call x1, Pallas kernels, gates(): pl.pallas_call(gate_kernel, in_specs=[hbm] * 4, out_specs=hbm, out_shape=...  11.4 us
    pallas_call x1, Pallas kernels, edges(): pl.pallas_call(edges_kernel, in_specs=[hbm] * 4, out_specs=vmem, out_shap...  8.68 us
    all_to_all x1, starting transfers between devices, shards(): lax.all_to_all(triangle(both_all), BACK_ORDER, split_axis=0, concat_axis=...  7.12 us
    pallas_call x1, Pallas kernels, finish(): pl.pallas_call(finish_kernel, in_specs=[vmem, hbm, hbm, hbm, hbm], out_sp...  6.83 us
    pallas_call x1, Pallas kernels, triangle(): pl.pallas_call(triangle_kernel, in_specs=[vmem], out_specs=pl.BlockSpec(m...  6.17 us
  transfers between devices with their start and end apart: 1, of which 1 were waited for; matrix products, arithmetic and copies ran while one was open for 0% of the time, Pallas kernels for 7%

profile of v7, /device:TPU:1, one launch (start us, length us, event | category | flops | bytes accessed | tf_op | source)
XLA Modules:
  0.0 160.0 jit_solution(16352904178459950535)
XLA Ops:
  0.0 8.7 %edges.1 = bf16[128,200,128]{2,1,0:T(8,128)(2,1)S(1)} custom-call(bf16[160,80,128]{2,1,0:T(8,128)(2,1)} %pair_ref.3, f32[1,128]{1,0:T(1,128)} %bitcast.4, f32[1,128]{1,0:T(1,128)} %bitcast.6, bf16[128,512]{1,0:T(8,128)(2,1)} %weight_hbm.3), custom_call_target="tpu_custom_call" | custom-call | flops 1677721600 | bytes 10485760 | tf_op jit(solution)/shard_map/edges/pallas_call | solution.py:139
  8.7 88.1 %all_to_all.10.edges_ref = bf16[128,200,128]{2,1,0:T(8,128)(2,1)S(1)} all-to-all(bf16[128,200,128]{2,1,0:T(8,128)(2,1)S(1)} %edges.1), channel_id=1, replica_groups=mesh['y'=4,'z_lo'=2,'core'=2,'z_hi'=2,'x'=4] {'z_hi','x','core','y','z_lo'}, dimensions={0} | all-to-all | bytes 13107200 | tf_op jit(solution)/shard_map/all_to_all | solution.py:380
  96.8 6.2 %triangle.1 = bf16[128,104,128]{2,1,0:T(8,128)(2,1)} custom-call(bf16[128,200,128]{2,1,0:T(8,128)(2,1)S(1)} %all_to_all.10.edges_ref), custom_call_target="tpu_custom_call" | custom-call | flops 4194304000 | bytes 10485760 | tf_op jit(solution)/shard_map/triangle/pallas_call | solution.py:268
  103.0 7.1 %all-to-all-start.1 = ((bf16[128,104,128]{2,1,0:T(8,128)(2,1)}), bf16[128,104,128]{2,1,0:T(8,128)(2,1)S(1)}, u32[]{:S(2)}, u32[]{:S(2)}) async-start(bf16[128,104,128]{2,1,0:T(8,128)(2,1)} %triangle.1), calls=%async_computation.1 | async-start | bytes 6815744 | tf_op jit(solution)/shard_map/all_to_all | solution.py:382
  110.1 11.4 %gates.1.gate_hbm = bf16[160,80,128]{2,1,0:T(8,128)(2,1)} custom-call(bf16[160,80,128]{2,1,0:T(8,128)(2,1)} %pair_ref.3, f32[1,128]{1,0:T(1,128)} %bitcast.5, f32[1,128]{1,0:T(1,128)} %bitcast.7, bf16[128,128]{1,0:T(8,128)(2,1)} %weight_hbm.4), custom_call_target="tpu_custom_call" | custom-call | flops 419430400 | bytes 31457280 | tf_op jit(solution)/shard_map/gates/pallas_call | solution.py:184
  121.5 31.6 %all-to-all-done.1.held = bf16[128,104,128]{2,1,0:T(8,128)(2,1)S(1)} async-done(((bf16[128,104,128]{2,1,0:T(8,128)(2,1)}), bf16[128,104,128]{2,1,0:T(8,128)(2,1)S(1)}, u32[]{:S(2)}, u32[]{:S(2)}) %all-to-all-start.1) | async-done | bytes 3407904 | tf_op jit(solution)/shard_map/all_to_all | solution.py:382
  153.1 6.8 %finish.1 = bf16[160,80,128]{2,1,0:T(8,128)(2,1)} custom-call(bf16[128,104,128]{2,1,0:T(8,128)(2,1)S(1)} %all-to-all-done.1.held, bf16[160,80,128]{2,1,0:T(8,128)(2,1)} %gates.1.gate_hbm, f32[1,128]{1,0:T(1,128)} %bitcast.8, f32[1,128]{1,0:T(1,128)} %bitcast.9, bf16[128,128]{1,0:T(8,128)(2,1)} %weight_hbm.5), custom_call_target="tpu_custom_call" | custom-call | flops 419430400 | bytes 10485760 | tf_op jit(solution)/shard_map/finish/pallas_call | solution.py:355
Async XLA Ops:
  103.0 50.1 %all-to-all-start.1 = ((bf16[128,104,128]{2,1,0:T(8,128)(2,1)}), bf16[128,104,128]{2,1,0:T(8,128)(2,1)S(1)}, u32[]{:S(2)}, u32[]{:S(2)}) async-start(bf16[128,104,128]{2,1,0:T(8,128)(2,1)} %triangle.1), calls=%async_computation.1 | async-start | bytes 6815744 | tf_op jit(solution)/shard_map/all_to_all | solution.py:382

commit v8 on v7

--- a/solution.py
+++ b/solution.py
@@ -290,13 +290,13 @@
     sems, small_sems
 ):
     def store(t):
-        rows = pl.ds(pl.multiple_of(t * CHUNK, CHUNK), CHUNK)
+        rows = pl.ds(t * CHUNK, CHUNK)
         return pltpu.make_async_copy(
             done.at[pl.ds(0, LANES), rows, :], out_ref.at[pl.ds(0, LANES), rows, :], sems.at[CHUNKS + 1]
         )
 
     def load(t):
-        rows = pl.ds(pl.multiple_of(t * CHUNK, CHUNK), CHUNK)
+        rows = pl.ds(t * CHUNK, CHUNK)
         return pltpu.make_async_copy(
             gate_hbm.at[pl.ds(0, LANES), rows, :], gate_ref.at[pl.ds(0, LANES), rows, :], sems.at[t]
         )
@@ -309,19 +309,19 @@
         load(t).start()
     turn = lax.axis_index("x")
     for h in range(C):
-        wide[h * STEP : h * STEP + TAIL, :] = held[h, COLS:, :].astype(F32)[:TAIL]
+        wide[1, h * STEP : h * STEP + TAIL, :] = held[h, COLS:, :].astype(F32)[:TAIL]
     for copy in small:
         copy.wait()
     gain = jnp.broadcast_to(gain_ref[...], (LANES, C)).T
     bias = jnp.broadcast_to(bias_ref[...], (LANES, C)).T
     weight = weight_ref[...]
 
-    def project(g):
-        normed = layer_norm(wide[pl.ds(g, C, stride=STEP), :], gain, bias, 0).astype(BF16)
+    def project(g, slot):
+        normed = layer_norm(wide[slot, pl.ds(g, C, stride=STEP), :], gain, bias, 0).astype(BF16)
         return lax.dot_general(normed, weight, (((0,), (0,)), ((), ())), preferred_element_type=F32)
 
     for m in range(TAIL):
-        value = project(m)
+        value = project(m, 1)
         for g in range(PACK):
             at = PACK * m + lax.rem(g + PACK - turn, PACK)
             tail[pl.ds(at, REST, stride=COLS_STEP), :] = value[g * REST : (g + 1) * REST]
@@ -332,17 +332,16 @@
     last = pltpu.make_async_copy(done.at[rest], out_ref.at[rest], sems.at[CHUNKS + 2])
     last.start()
 
-    @pl.loop(0, CHUNKS)
-    def _(t):
+    for t in range(CHUNKS):
+        to, slot = t * CHUNK, t % 2
+        for h in range(C):
+            wide[slot, h * STEP : h * STEP + CHUNK, :] = held[h, pl.ds(to, CHUNK), :].astype(F32)
+        for g in range(CHUNK):
+            dense[slot, pl.ds(g, LANES, stride=STEP), :] = project(g, slot)
         load(t).wait()
-        to = pl.multiple_of(t * CHUNK, CHUNK)
-        for h in range(C):
-            wide[h * STEP : h * STEP + CHUNK, :] = held[h, pl.ds(to, CHUNK), :].astype(F32)
-        for g in range(CHUNK):
-            dense[pl.ds(g, LANES, stride=STEP), :] = project(g)
         for i in range(LANES):
             gate = gate_ref[i, pl.ds(to, CHUNK), :].astype(F32)
-            done[i, pl.ds(to, CHUNK), :] = (gate * dense[i * STEP : i * STEP + CHUNK, :]).astype(BF16)
+            done[i, pl.ds(to, CHUNK), :] = (gate * dense[slot, i * STEP : i * STEP + CHUNK, :]).astype(BF16)
         store(t).start()
 
     last.wait()
@@ -362,8 +361,8 @@
             pltpu.VMEM((1, C), F32),
             pltpu.VMEM((1, C), F32),
             pltpu.VMEM((C, C), BF16),
-            pltpu.VMEM((C * STEP + SPARE, LANES), F32),
-            pltpu.VMEM((LANES * STEP, C), F32),
+            pltpu.VMEM((2, C * STEP + SPARE, LANES), F32),
+            pltpu.VMEM((2, LANES * STEP, C), F32),
             pltpu.VMEM((REST * COLS_STEP, C), F32),
             pltpu.VMEM((ROWS, COLS, C), BF16),
             pltpu.SemaphoreType.DMA((CHUNKS + 3,)),

time: 160 us -> 160 us (level)
  no operation moved by 1% of the time
where the time goes in v8:
time: 160 us
  blocking collectives  88.1 us (55%)
  Pallas kernels  32.7 us (20%)
  waiting for transfers between devices  31.6 us (20%)
  starting transfers between devices  7.12 us (4%)
    all_to_all x1, blocking collectives, shards(): lax.all_to_all(both, OUT_ORDER, split_axis=0, concat_axis=0, tiled=True)  88.1 us
    all_to_all x1, waiting for transfers between devices, shards(): lax.all_to_all(triangle(both_all), BACK_ORDER, split_axis=0, concat_axis=...  31.6 us
    pallas_call x1, Pallas kernels, gates(): pl.pallas_call(gate_kernel, in_specs=[hbm] * 4, out_specs=hbm, out_shape=...  11.4 us
    pallas_call x1, Pallas kernels, edges(): pl.pallas_call(edges_kernel, in_specs=[hbm] * 4, out_specs=vmem, out_shap...  8.68 us
    all_to_all x1, starting transfers between devices, shards(): lax.all_to_all(triangle(both_all), BACK_ORDER, split_axis=0, concat_axis=...  7.12 us
    pallas_call x1, Pallas kernels, finish(): pl.pallas_call(finish_kernel, in_specs=[vmem, hbm, hbm, hbm, hbm], out_sp...  6.46 us
    pallas_call x1, Pallas kernels, triangle(): pl.pallas_call(triangle_kernel, in_specs=[vmem], out_specs=pl.BlockSpec(m...  6.17 us
  transfers between devices with their start and end apart: 1, of which 1 were waited for; matrix products, arithmetic and copies ran while one was open for 0% of the time, Pallas kernels for 7%

profile of v8, /device:TPU:1, one launch (start us, length us, event | category | flops | bytes accessed | tf_op | source)
XLA Modules:
  0.0 159.6 jit_solution(13271072085457530015)
XLA Ops:
  0.0 8.7 %edges.1 = bf16[128,200,128]{2,1,0:T(8,128)(2,1)S(1)} custom-call(bf16[160,80,128]{2,1,0:T(8,128)(2,1)} %pair_ref.3, f32[1,128]{1,0:T(1,128)} %bitcast.4, f32[1,128]{1,0:T(1,128)} %bitcast.6, bf16[128,512]{1,0:T(8,128)(2,1)} %weight_hbm.3), custom_call_target="tpu_custom_call" | custom-call | flops 1677721600 | bytes 10485760 | tf_op jit(solution)/shard_map/edges/pallas_call | solution.py:139
  8.7 88.1 %all_to_all.10.edges_ref = bf16[128,200,128]{2,1,0:T(8,128)(2,1)S(1)} all-to-all(bf16[128,200,128]{2,1,0:T(8,128)(2,1)S(1)} %edges.1), channel_id=1, replica_groups=mesh['y'=4,'z_lo'=2,'core'=2,'z_hi'=2,'x'=4] {'z_hi','x','core','y','z_lo'}, dimensions={0} | all-to-all | bytes 13107200 | tf_op jit(solution)/shard_map/all_to_all | solution.py:379
  96.8 6.2 %triangle.1 = bf16[128,104,128]{2,1,0:T(8,128)(2,1)} custom-call(bf16[128,200,128]{2,1,0:T(8,128)(2,1)S(1)} %all_to_all.10.edges_ref), custom_call_target="tpu_custom_call" | custom-call | flops 4194304000 | bytes 10485760 | tf_op jit(solution)/shard_map/triangle/pallas_call | solution.py:268
  103.0 7.1 %all-to-all-start.1 = ((bf16[128,104,128]{2,1,0:T(8,128)(2,1)}), bf16[128,104,128]{2,1,0:T(8,128)(2,1)S(1)}, u32[]{:S(2)}, u32[]{:S(2)}) async-start(bf16[128,104,128]{2,1,0:T(8,128)(2,1)} %triangle.1), calls=%async_computation.1 | async-start | bytes 6815744 | tf_op jit(solution)/shard_map/all_to_all | solution.py:381
  110.1 11.4 %gates.1.gate_hbm = bf16[160,80,128]{2,1,0:T(8,128)(2,1)} custom-call(bf16[160,80,128]{2,1,0:T(8,128)(2,1)} %pair_ref.3, f32[1,128]{1,0:T(1,128)} %bitcast.5, f32[1,128]{1,0:T(1,128)} %bitcast.7, bf16[128,128]{1,0:T(8,128)(2,1)} %weight_hbm.4), custom_call_target="tpu_custom_call" | custom-call | flops 419430400 | bytes 31457280 | tf_op jit(solution)/shard_map/gates/pallas_call | solution.py:184
  121.5 31.6 %all-to-all-done.1.held = bf16[128,104,128]{2,1,0:T(8,128)(2,1)S(1)} async-done(((bf16[128,104,128]{2,1,0:T(8,128)(2,1)}), bf16[128,104,128]{2,1,0:T(8,128)(2,1)S(1)}, u32[]{:S(2)}, u32[]{:S(2)}) %all-to-all-start.1) | async-done | bytes 3407904 | tf_op jit(solution)/shard_map/all_to_all | solution.py:381
  153.1 6.5 %finish.1 = bf16[160,80,128]{2,1,0:T(8,128)(2,1)} custom-call(bf16[128,104,128]{2,1,0:T(8,128)(2,1)S(1)} %all-to-all-done.1.held, bf16[160,80,128]{2,1,0:T(8,128)(2,1)} %gates.1.gate_hbm, f32[1,128]{1,0:T(1,128)} %bitcast.8, f32[1,128]{1,0:T(1,128)} %bitcast.9, bf16[128,128]{1,0:T(8,128)(2,1)} %weight_hbm.5), custom_call_target="tpu_custom_call" | custom-call | flops 419430400 | bytes 10485760 | tf_op jit(solution)/shard_map/finish/pallas_call | solution.py:354
Async XLA Ops:
  103.0 50.1 %all-to-all-start.1 = ((bf16[128,104,128]{2,1,0:T(8,128)(2,1)}), bf16[128,104,128]{2,1,0:T(8,128)(2,1)S(1)}, u32[]{:S(2)}, u32[]{:S(2)}) async-start(bf16[128,104,128]{2,1,0:T(8,128)(2,1)} %triangle.1), calls=%async_computation.1 | async-start | bytes 6815744 | tf_op jit(solution)/shard_map/all_to_all | solution.py:381
